TPU v7x, 32 devices: a whole 2x2x4 slice. The times are simulated.
32 devices in a mesh: gx: 2 (over y), gy: 2 (over core), vert: 8 (over z, x).
Axes of the slice: x: 2, y: 2, z: 4, core: 2. Of those that a mesh axis runs over, the one named last changes fastest.
Arguments:
- distribution: float32 [8000, 64, 256], P('vert', 'gx', 'gy'), may hold values from 0 to 13, as said below
- collision_rate: float32 [64, 256], P('gx', 'gy'), may hold values from 0.05 to 0.9
Outputs:
- advanced: float32 [8000, 64, 256], P('vert', 'gx', 'gy')
Inputs may be any that keep to these rules, and one draw needn't show every extreme that they name: `distribution`: Nonnegative, of the shape of a local equilibrium with cell-to-cell variation.
All inputs are finite; a program needn't handle non-finite values.
Results may differ from a plain program's by a relative error of at most 0.0003.
Values sent between devices are 32-bit elements; how exact they have to be, the bound alone decides.
A program may use at most 384 MiB of HBM per device.

v0:
```python
import math

import jax
import jax.numpy as jnp
from jax import lax
from jax.sharding import PartitionSpec as P

VG = 20
NZ = 2
STEPS = 2


speed_max = 4.5
time_step = 0.3 / 4.5


def with_halo(cells, sides, width):
    for axis, dim in sides:
        count = lax.axis_size(axis)
        head = lax.slice_in_dim(cells, 0, width, axis=dim)
        tail = lax.slice_in_dim(cells, cells.shape[dim] - width, cells.shape[dim], axis=dim)
        cells = jnp.concatenate(
            [
                lax.ppermute(tail, axis, [(i, (i + 1) % count) for i in range(count)]),
                cells,
                lax.ppermute(head, axis, [((i + 1) % count, i) for i in range(count)]),
            ],
            axis=dim,
        )
    return cells


def grid_speed(index):
    return speed_max * (2.0 * (index.astype(jnp.float32) + 0.5) / VG - 1.0)


def velocity_tables(first, count):
    labels = first + jnp.arange(count, dtype=jnp.int32)
    speed_x = grid_speed(labels // (VG * VG))
    speed_y = grid_speed(labels // VG % VG)
    speed_z = grid_speed(labels % VG)
    weight = (2.0 * speed_max / VG) ** 3 / (2.0 * math.pi) ** 1.5
    table = jnp.stack(
        [
            weight * jnp.ones_like(speed_x),
            weight * speed_x,
            weight * speed_y,
            weight * speed_z,
            weight * (speed_x * speed_x + speed_y * speed_y + speed_z * speed_z),
        ]
    )
    return (speed_x, speed_y, speed_z, table)


def running(center, xpad, ypad, speed_x, speed_y, speed_z):
    cols = center.shape[2]
    shaped = (-1, 1, 1)
    speed_x = speed_x.reshape(shaped)
    speed_y = speed_y.reshape(shaped)
    speed_z = speed_z.reshape(shaped)
    plane = lax.broadcasted_iota(jnp.int32, (1, 1, cols), 2) % NZ

    def below(offset):
        return jnp.where(
            plane >= offset, jnp.roll(center, offset, 2), jnp.roll(center, offset - NZ, 2)
        )

    def above(offset):
        return jnp.where(
            plane < NZ - offset, jnp.roll(center, -offset, 2), jnp.roll(center, NZ - offset, 2)
        )

    back_x = (3.0 * center - 4.0 * xpad[:, 1:-3] + xpad[:, :-4]) * 0.5
    ahead_x = (-3.0 * center + 4.0 * xpad[:, 3:-1] - xpad[:, 4:]) * 0.5
    back_y = (3.0 * center - 4.0 * ypad[:, :, NZ : NZ + cols] + ypad[:, :, :cols]) * 0.5
    ahead_y = (
        -3.0 * center
        + 4.0 * ypad[:, :, 3 * NZ : 3 * NZ + cols]
        - ypad[:, :, 4 * NZ : 4 * NZ + cols]
    ) * 0.5
    back_z = (3.0 * center - 4.0 * below(1) + below(2)) * 0.5
    ahead_z = (-3.0 * center + 4.0 * above(1) - above(2)) * 0.5
    flux = jnp.maximum(speed_x, 0.0) * back_x + jnp.minimum(speed_x, 0.0) * ahead_x
    flux = flux + jnp.maximum(speed_y, 0.0) * back_y + jnp.minimum(speed_y, 0.0) * ahead_y
    flux = flux + jnp.maximum(speed_z, 0.0) * back_z + jnp.minimum(speed_z, 0.0) * ahead_z
    return center - time_step * flux


def parameters(moments):
    density = moments[0]
    flow_x = moments[1] / density
    flow_y = moments[2] / density
    flow_z = moments[3] / density
    temper = (moments[4] / density - (flow_x * flow_x + flow_y * flow_y + flow_z * flow_z)) / 3.0
    return jnp.stack([density / (temper * jnp.sqrt(temper)), flow_x, flow_y, flow_z, 0.5 / temper])


def relax(moved, speed_x, speed_y, speed_z, params, rate):
    diff_x = speed_x[:, None] - params[1][None]
    diff_y = speed_y[:, None] - params[2][None]
    diff_z = speed_z[:, None] - params[3][None]
    maxwell = params[0][None] * jnp.exp(
        -params[4][None] * (diff_x * diff_x + diff_y * diff_y + diff_z * diff_z)
    )
    return moved + rate[None] * (maxwell - moved)


def body(distribution, collision_rate):
    vel_local, rows_x, cols_yz = distribution.shape
    first = lax.axis_index("vert") * vel_local
    speed_x, speed_y, speed_z, table = velocity_tables(first, vel_local)
    rate = collision_rate.reshape(-1)
    state = distribution
    for step in range(STEPS):
        xpad = with_halo(state, (("gx", 1),), 2)
        ypad = with_halo(state, (("gy", 2),), 2 * NZ)
        moved = running(state, xpad, ypad, speed_x, speed_y, speed_z)
        moved = moved.reshape(vel_local, -1)
        partial_sum = jnp.dot(table, moved, precision=lax.Precision.HIGHEST)
        params = parameters(lax.psum(partial_sum, "vert"))
        state = relax(moved, speed_x, speed_y, speed_z, params, rate).reshape(
            vel_local, rows_x, cols_yz
        )
    return state


def solution(mesh):
    placed = (P("vert", "gx", "gy"), P("gx", "gy"))
    return jax.shard_map(
        body, mesh=mesh, in_specs=placed, out_specs=P("vert", "gx", "gy"), check_vma=False
    )
```

profile of v0, /device:TPU:0, one launch (start us, length us, event | category | flops | bytes accessed | tf_op | source)
XLA Modules:
  0.0 770.9 jit_solution(1926105677055258414)
XLA Ops:
  6.5 9.6 %copy.53 = f32[1000,32,128]{2,0,1:T(8,128)S(1)} copy(f32[1000,32,128]{2,1,0:T(8,128)} %param.2) | data formatting | bytes 32768000 | tf_op args[0]
  16.2 6.0 copy-done.1
  22.2 1.1 fusion.105
  23.3 3.0 collective-permute-start
  26.3 0.0 collective-permute-start.1
  26.3 12.0 %fusion.106 = (f32[1000,32,4]{2,1,0:T(8,128)}, f32[1000,32,4]{2,1,0:T(8,128)}) fusion(f32[1000,32,128]{2,1,0:T(8,128)S(1)} %copy-done.2), kind=kLoop, calls=%fused_computation.184 | loop fusion | bytes 2048000 | tf_op jit(solution)/shard_map/slice | solution.py:21
  38.3 10.6 %copy.61 = f32[1000,32,4]{0,1,2:T(8,128)} copy(f32[1000,32,4]{2,1,0:T(8,128)} %get-tuple-element.39) | data formatting | bytes 1024000
  48.9 10.6 %copy.62 = f32[1000,32,4]{0,1,2:T(8,128)} copy(f32[1000,32,4]{2,1,0:T(8,128)} %get-tuple-element.40) | data formatting | bytes 1024000
  59.6 0.5 collective-permute-start.3
  60.1 24.4 %fusion.101 = (f32[1000,32,1]{2,0,1:T(8,128)}, f32[1000,32,1]{2,0,1:T(8,128)}) fusion(f32[1000,32,128]{2,0,1:T(8,128)} %copy-done.1), kind=kLoop, calls=%fused_computation.179 | loop fusion | bytes 512000 | tf_op jit(solution)/shard_map/jit(_roll_static)/slice | solution.py:65
  84.5 23.2 %fusion.102 = (f32[1000,32,127]{2,0,1:T(8,128)}, f32[1000,32,127]{2,0,1:T(8,128)}) fusion(f32[1000,32,128]{2,0,1:T(8,128)} %copy-done.1), kind=kLoop, calls=%fused_computation.180 | loop fusion | bytes 65024000 | tf_op jit(solution)/shard_map/jit(_roll_static)/slice | solution.py:65
  107.8 12.0 %fusion.103 = (f32[1000,32,126]{2,0,1:T(8,128)}, f32[1000,32,126]{2,0,1:T(8,128)}) fusion(f32[1000,32,128]{2,0,1:T(8,128)S(1)} %bitcast.17), kind=kLoop, calls=%fused_computation.181 | loop fusion | bytes 64512000 | tf_op jit(solution)/shard_map/jit(_roll_static)/slice | solution.py:70
  119.7 12.1 %fusion.104 = (f32[1000,32,2]{2,0,1:T(8,128)}, f32[1000,32,2]{2,0,1:T(8,128)}) fusion(f32[1000,32,128]{2,0,1:T(8,128)S(1)} %bitcast.17), kind=kLoop, calls=%fused_computation.182 | loop fusion | bytes 1024000 | tf_op jit(solution)/shard_map/jit(_roll_static)/slice | solution.py:70
  131.8 0.1 add_multiply_fusion
  131.9 0.1 broadcast_multiply_fusion.1
  132.2 9.6 %copy.38 = f32[1000,32,4]{2,0,1:T(8,128)} copy(f32[1000,32,4]{0,1,2:T(8,128)} %collective-permute-done.2) | data formatting | bytes 1024000 | tf_op jit(solution)/shard_map/ppermute | solution.py:24
  141.8 9.7 %copy.42 = f32[1000,32,4]{2,0,1:T(8,128)} copy(f32[1000,32,4]{0,1,2:T(8,128)} %collective-permute-done.3) | data formatting | bytes 1024000 | tf_op jit(solution)/shard_map/ppermute | solution.py:26
  151.5 1.0 constant_dynamic-update-slice_fusion.1
  152.5 18.5 %constant_dynamic-update-slice_fusion = (f32[1000,34,128]{2,0,1:T(8,128)}, f32[1000,34,128]{2,0,1:T(8,128)}) fusion(f32[1000,34,128]{2,0,1:T(8,128)} %constant_dynamic-update-slice_fusion.1, f32[1000,32,128]{2,1,0:T(8,128)} %param.2), kind=kLoop, calls=%fused_computation.114 | loop fusion | bytes 49152000 | tf_op jit(solution)/shard_map/concatenate | solution.py:22
  171.0 1.1 constant_dynamic-update-slice_fusion.2
  172.1 111.8 %fusion.40 = f32[1000,32,128]{2,0,1:T(8,128)} fusion(f32[1000,32,128]{2,0,1:T(8,128)} %copy-done.1, f32[1000,32,4]{2,0,1:T(8,128)} %copy.42, f32[1000,32,4]{2,0,1:T(8,128)} %copy.38, f32[1000,34,128]{2,0,1:T(8,128)} %constant_dynamic-update-slice_fusion.2, f32[1000,34,128]{2,0,1:T(8,128)} %get-tuple-element.35, f32[1000,32,126]{2,0,1:T(8,128)} %get-tuple-element.32, ...), kind=kLoop, calls=%fused_computation.54 | loop fusion | flops 184320000 | bytes 164888512 | tf_op jit(solution)/shard_map/sub | solution.py:86
  283.9 17.4 %copy.54 = f32[1000,32,128]{0,2,1:T(8,128)} copy(f32[1000,32,128]{2,0,1:T(8,128)} %fusion.40) | data formatting | bytes 32768000 | tf_op jit(solution)/shard_map/sub | solution.py:86
  301.3 17.8 %fusion.107 = f32[5,4096]{1,0:T(8,128)} fusion(f32[5,1000]{1,0:T(8,128)S(1)} %stack.5, f32[1000,4096]{0,1:T(8,128)} %bitcast.19), kind=kOutput, calls=%fused_computation.185 | convolution fusion | flops 245760000 | bytes 16485920 | tf_op jit(solution)/shard_map/dot_general | solution.py:119
  319.1 0.0 all-reduce.5.cloned.1.call-start
  319.2 71.5 %all-reduce.3.cloned.1.call-done = f32[5,4096]{1,0:T(8,128)} async-done(((f32[5,4096]{1,0:T(8,128)}), f32[5,4096]{1,0:T(8,128)}) %all-reduce.3.cloned.1.call-update) | async-done | bytes 81936 | tf_op jit(solution)/shard_map/psum | solution.py:120
  390.7 1.5 fusion.56
  392.3 11.5 %multiply_add_fusion.3 = f32[1000,32,128]{2,0,1:T(8,128)S(1)} fusion(f32[1000,32,128]{2,0,1:T(8,128)} %fusion.40, f32[32,128]{1,0:T(8,128)S(1)} %bitcast.27, f32[1000]{0:T(1024)S(1)} %get-tuple-element.43, f32[32,128]{1,0:T(8,128)S(1)} %bitcast.26, f32[1000]{0:T(1024)S(1)} %get-tuple-element.42, f32[32,128]{1,0:T(8,128)S(1)} %bitcast.25, ...), kind=kLoop, calls=%fused_computation.91 | loop fusion | flops 53248000 | bytes 32878304 | tf_op jit(solution)/shard_map/add | solution.py:105
  403.8 13.4 %fusion.99 = (f32[1000,32,4]{2,0,1:T(8,128)}, f32[1000,32,4]{2,0,1:T(8,128)}) fusion(f32[1000,32,128]{2,0,1:T(8,128)S(1)} %multiply_add_fusion.3), kind=kLoop, calls=%fused_computation.177 | loop fusion | bytes 2048000 | tf_op jit(solution)/shard_map/slice | solution.py:21
  417.2 12.7 %fusion.95 = (f32[1000,32,1]{2,0,1:T(8,128)}, f32[1000,32,1]{2,0,1:T(8,128)}) fusion(f32[1000,32,128]{2,0,1:T(8,128)S(1)} %multiply_add_fusion.3), kind=kLoop, calls=%fused_computation.173 | loop fusion | bytes 512000 | tf_op jit(solution)/shard_map/jit(_roll_static)/slice | solution.py:65
  429.8 12.2 %fusion.96 = (f32[1000,32,127]{2,0,1:T(8,128)}, f32[1000,32,127]{2,0,1:T(8,128)}) fusion(f32[1000,32,128]{2,0,1:T(8,128)S(1)} %multiply_add_fusion.3), kind=kLoop, calls=%fused_computation.174 | loop fusion | bytes 65024000 | tf_op jit(solution)/shard_map/jit(_roll_static)/slice | solution.py:65
  442.1 11.9 %fusion.97 = (f32[1000,32,126]{2,0,1:T(8,128)}, f32[1000,32,126]{2,0,1:T(8,128)}) fusion(f32[1000,32,128]{2,0,1:T(8,128)S(1)} %multiply_add_fusion.3), kind=kLoop, calls=%fused_computation.175 | loop fusion | bytes 64512000 | tf_op jit(solution)/shard_map/jit(_roll_static)/slice | solution.py:70
  454.0 0.1 fusion.100
  454.1 10.6 %copy.55 = f32[1000,32,4]{0,1,2:T(8,128)} copy(f32[1000,32,4]{2,0,1:T(8,128)} %get-tuple-element.23) | data formatting | bytes 1024000 | tf_op jit(solution)/shard_map/slice | solution.py:21
  464.7 10.6 %copy.57 = f32[1000,32,4]{0,1,2:T(8,128)} copy(f32[1000,32,4]{2,0,1:T(8,128)} %get-tuple-element.24) | data formatting | bytes 1024000 | tf_op jit(solution)/shard_map/slice | solution.py:20
  475.3 0.5 collective-permute-start.7
  475.8 1.5 collective-permute-start.4
  477.3 0.6 collective-permute-start.5
  477.8 23.1 %fusion.98 = (f32[1000,32,2]{2,0,1:T(8,128)}, f32[1000,32,2]{2,0,1:T(8,128)}) fusion(f32[1000,32,128]{2,0,1:T(8,128)} %copy-done), kind=kLoop, calls=%fused_computation.176 | loop fusion | bytes 1024000 | tf_op jit(solution)/shard_map/jit(_roll_static)/slice | solution.py:70
  500.9 9.8 %copy.56 = f32[1000,32,4]{2,0,1:T(8,128)} copy(f32[1000,32,4]{0,1,2:T(8,128)} %collective-permute-done.6) | data formatting | bytes 1024000 | tf_op jit(solution)/shard_map/ppermute | solution.py:24
  510.7 9.6 %copy.58 = f32[1000,32,4]{2,0,1:T(8,128)} copy(f32[1000,32,4]{0,1,2:T(8,128)} %collective-permute-done.7) | data formatting | bytes 1024000 | tf_op jit(solution)/shard_map/ppermute | solution.py:26
  520.4 2.1 collective-permute-done.5
  522.4 114.3 %fusion.11 = f32[1000,32,128]{2,0,1:T(8,128)} fusion(f32[1000,32,128]{2,0,1:T(8,128)} %copy-done, f32[1000,2,128]{2,0,1:T(8,128)} %collective-permute-done.5, f32[1000,2,128]{2,0,1:T(8,128)S(1)} %collective-permute-done.4, f32[1000,32,4]{2,0,1:T(8,128)} %copy.58, f32[1000,32,4]{2,0,1:T(8,128)} %copy.56, f32[1000,32,126]{2,0,1:T(8,128)} %get-tuple-element.20, ...), kind=kLoop, calls=%fused_computation.23 | loop fusion | flops 200704000 | bytes 101400512 | tf_op jit(solution)/shard_map/sub | solution.py:86
  636.7 17.4 %copy.59 = f32[1000,32,128]{0,2,1:T(8,128)} copy(f32[1000,32,128]{2,0,1:T(8,128)} %fusion.11) | data formatting | bytes 32768000 | tf_op jit(solution)/shard_map/sub | solution.py:86
  654.1 17.8 %fusion.108 = f32[5,4096]{1,0:T(8,128)} fusion(f32[5,1000]{1,0:T(8,128)S(1)} %copy-done.4, f32[1000,4096]{0,1:T(8,128)} %bitcast.18), kind=kOutput, calls=%fused_computation.186 | convolution fusion | flops 245760000 | bytes 16485920 | tf_op jit(solution)/shard_map/dot_general | solution.py:119
  671.9 69.1 %all-reduce.5.cloned.1.call-done = f32[5,4096]{1,0:T(8,128)} async-done(((f32[5,4096]{1,0:T(8,128)}), f32[5,4096]{1,0:T(8,128)}) %all-reduce.5.cloned.1.call-update) | async-done | bytes 81936 | tf_op jit(solution)/shard_map/psum | solution.py:120
  741.0 1.5 fusion.57
  742.6 11.2 %multiply_add_fusion.2 = f32[1000,32,128]{2,0,1:T(8,128)S(1)} fusion(f32[1000,32,128]{2,0,1:T(8,128)} %fusion.11, f32[32,128]{1,0:T(8,128)S(1)} %bitcast.23, f32[32,128]{1,0:T(8,128)S(1)} %bitcast.22, f32[32,128]{1,0:T(8,128)S(1)} %bitcast.21, f32[32,128]{1,0:T(8,128)S(1)} %bitcast.28, f32[32,128]{1,0:T(8,128)S(1)} %bitcast.20, f32[1000]{0:T(1024)S(1)} %copy-done.8, ...), kind=kLoop, calls=%fused_computation.90 | loop fusion | flops 53248000 | bytes 32878304 | tf_op jit(solution)/shard_map/add | solution.py:105
  753.9 9.8 %copy.60 = f32[1000,32,128]{2,1,0:T(8,128)} copy(f32[1000,32,128]{2,0,1:T(8,128)S(1)} %multiply_add_fusion.2) | data formatting | bytes 32768000 | tf_op jit(solution)/shard_map/add | solution.py:105
  (57 shorter events, 0.4 us)
Async XLA Ops:
  6.5 384.2 %all-reduce.3.cloned.1.call-start = ((), (), s32[]{:S(2)}) async-start(), calls=%async_computation | async-start | bytes 262144 | tf_op jit(solution)/shard_map/psum | solution.py:120
  6.5 19.8 %copy-start.2 = (f32[1000,32,128]{2,1,0:T(8,128)S(1)}, f32[1000,32,128]{2,1,0:T(8,128)}, u32[]{:S(2)}) copy-start(f32[1000,32,128]{2,1,0:T(8,128)} %param.2) | copy-start | bytes 49152004
  16.2 6.0 copy-start.1
  23.3 128.2 %collective-permute-start = (f32[1000,2,128]{2,0,1:T(8,128)}, f32[1000,2,128]{2,0,1:T(8,128)S(1)}, u32[]{:S(2)}, u32[]{:S(2)}) collective-permute-start(f32[1000,2,128]{2,0,1:T(8,128)} %get-tuple-element.37), channel_id=1, source_target_pairs={{0,16},{16,0},{1,17},{17,1},{2,18},{18,2},{3,19},{19,3},{4,20},{20... | collective-permute-start | bytes 3072008 | tf_op jit(solution)/shard_map/ppermute | solution.py:24
  26.3 144.7 %collective-permute-start.1 = (f32[1000,2,128]{2,0,1:T(8,128)S(1)}, f32[1000,2,128]{2,0,1:T(8,128)S(1)}, u32[]{:S(2)}, u32[]{:S(2)}) collective-permute-start(f32[1000,2,128]{2,0,1:T(8,128)S(1)} %get-tuple-element.38), channel_id=1, source_target_pairs={{16,0},{0,16},{17,1},{1,17},{18,2},{2,18},{19,3},{3,19},{20,4},{4,... | collective-permute-start | bytes 3072008 | tf_op jit(solution)/shard_map/ppermute | solution.py:26
  48.9 83.3 %collective-permute-start.2 = (f32[1000,32,4]{0,1,2:T(8,128)}, f32[1000,32,4]{0,1,2:T(8,128)}, u32[]{:S(2)}, u32[]{:S(2)}) collective-permute-start(f32[1000,32,4]{0,1,2:T(8,128)} %copy.61), channel_id=1, source_target_pairs={{0,8},{8,0},{1,9},{9,1},{2,10},{10,2},{3,11},{11,3},{4,12},{12,4},... | collective-permute-start | bytes 1536008 | tf_op jit(solution)/shard_map/ppermute | solution.py:24
  59.6 82.3 %collective-permute-start.3 = (f32[1000,32,4]{0,1,2:T(8,128)}, f32[1000,32,4]{0,1,2:T(8,128)}, u32[]{:S(2)}, u32[]{:S(2)}) collective-permute-start(f32[1000,32,4]{0,1,2:T(8,128)} %copy.62), channel_id=1, source_target_pairs={{8,0},{0,8},{9,1},{1,9},{10,2},{2,10},{11,3},{3,11},{12,4},{4,12},... | collective-permute-start | bytes 1536008 | tf_op jit(solution)/shard_map/ppermute | solution.py:26
  60.1 47.7 %slice-start = ((s8[16384000]{0:T(1024)(128)(4,1)}), s8[4194304]{0:T(1024)(128)(4,1)S(1)}, s32[]{:S(2)}) async-start(s8[16384000]{0:T(1024)(128)(4,1)} %bitcast.16), calls=%async_computation.2 | async-start | bytes 8388608
  60.1 47.7 %slice-start.1 = ((s8[16384000]{0:T(1024)(128)(4,1)}), s8[4194304]{0:T(1024)(128)(4,1)S(1)}, s32[]{:S(2)}) async-start(s8[16384000]{0:T(1024)(128)(4,1)} %bitcast.16), calls=%async_computation.3 | async-start | bytes 8388608
  60.1 47.7 %slice-start.2 = ((s8[16384000]{0:T(1024)(128)(4,1)}), s8[4194304]{0:T(1024)(128)(4,1)S(1)}, s32[]{:S(2)}) async-start(s8[16384000]{0:T(1024)(128)(4,1)} %bitcast.16), calls=%async_computation.4 | async-start | bytes 8388608
  84.5 23.3 %slice-start.3 = ((s8[16384000]{0:T(1024)(128)(4,1)}), s8[3801088]{0:T(1024)(128)(4,1)S(1)}, s32[]{:S(2)}) async-start(s8[16384000]{0:T(1024)(128)(4,1)} %bitcast.16), calls=%async_computation.5 | async-start | bytes 7602176
  132.0 169.2 %copy-start.3 = (f32[5,1000]{1,0:T(8,128)}, f32[5,1000]{1,0:T(8,128)S(1)}, u32[]{:S(2)}) copy-start(f32[5,1000]{1,0:T(8,128)S(1)} %stack.5) | copy-start | bytes 60004
  132.1 260.1 %copy-start.7 = (f32[1000]{0:T(1024)}, f32[1000]{0:T(1024)S(1)}, u32[]{:S(2)}) copy-start(f32[1000]{0:T(1024)S(1)} %get-tuple-element.43) | copy-start | bytes 12004
  301.3 91.0 %copy-start.5 = (f32[32,128]{1,0:T(8,128)S(1)}, f32[32,128]{1,0:T(8,128)}, u32[]{:S(2)}) copy-start(f32[32,128]{1,0:T(8,128)} %param.3) | copy-start | bytes 49156
  319.1 421.9 %all-reduce.5.cloned.1.call-start = ((), (), s32[]{:S(2)}) async-start(), calls=%async_computation.1 | async-start | bytes 262144 | tf_op jit(solution)/shard_map/psum | solution.py:120
  319.2 84.6 %copy-start.9 = (f32[1000]{0:T(1024)}, f32[1000]{0:T(1024)S(1)}, u32[]{:S(2)}) copy-start(f32[1000]{0:T(1024)S(1)} %get-tuple-element.41) | copy-start | bytes 12004
  319.2 84.6 %copy-start.11 = (f32[1000]{0:T(1024)}, f32[1000]{0:T(1024)S(1)}, u32[]{:S(2)}) copy-start(f32[1000]{0:T(1024)S(1)} %get-tuple-element.42) | copy-start | bytes 12004
  403.8 50.2 %copy-start = (f32[1000,32,128]{2,0,1:T(8,128)}, f32[1000,32,128]{2,0,1:T(8,128)S(1)}, u32[]{:S(2)}) copy-start(f32[1000,32,128]{2,0,1:T(8,128)S(1)} %multiply_add_fusion.3) | copy-start | bytes 49152004
  464.7 36.2 %collective-permute-start.6 = (f32[1000,32,4]{0,1,2:T(8,128)}, f32[1000,32,4]{0,1,2:T(8,128)}, u32[]{:S(2)}, u32[]{:S(2)}) collective-permute-start(f32[1000,32,4]{0,1,2:T(8,128)} %copy.55), channel_id=1, source_target_pairs={{0,8},{8,0},{1,9},{9,1},{2,10},{10,2},{3,11},{11,3},{4,12},{12,4},... | collective-permute-start | bytes 1536008 | tf_op jit(solution)/shard_map/ppermute | solution.py:24
  475.3 35.4 %collective-permute-start.7 = (f32[1000,32,4]{0,1,2:T(8,128)}, f32[1000,32,4]{0,1,2:T(8,128)}, u32[]{:S(2)}, u32[]{:S(2)}) collective-permute-start(f32[1000,32,4]{0,1,2:T(8,128)} %copy.57), channel_id=1, source_target_pairs={{8,0},{0,8},{9,1},{1,9},{10,2},{2,10},{11,3},{3,11},{12,4},{4,12},... | collective-permute-start | bytes 1536008 | tf_op jit(solution)/shard_map/ppermute | solution.py:26
  475.8 44.5 %collective-permute-start.4 = (f32[1000,2,128]{2,0,1:T(8,128)S(1)}, f32[1000,2,128]{2,0,1:T(8,128)S(1)}, u32[]{:S(2)}, u32[]{:S(2)}) collective-permute-start(f32[1000,2,128]{2,0,1:T(8,128)S(1)} %get-tuple-element.25), channel_id=1, source_target_pairs={{0,16},{16,0},{1,17},{17,1},{2,18},{18,2},{3,19},{19,3},{4,20},{20... | collective-permute-start | bytes 3072008 | tf_op jit(solution)/shard_map/ppermute | solution.py:24
  477.3 45.1 %collective-permute-start.5 = (f32[1000,2,128]{2,0,1:T(8,128)S(1)}, f32[1000,2,128]{2,0,1:T(8,128)}, u32[]{:S(2)}, u32[]{:S(2)}) collective-permute-start(f32[1000,2,128]{2,0,1:T(8,128)S(1)} %get-tuple-element.26), channel_id=1, source_target_pairs={{16,0},{0,16},{17,1},{1,17},{18,2},{2,18},{19,3},{3,19},{20,4},{4,... | collective-permute-start | bytes 3072008 | tf_op jit(solution)/shard_map/ppermute | solution.py:26
  636.7 17.4 %copy-start.4 = (f32[5,1000]{1,0:T(8,128)S(1)}, f32[5,1000]{1,0:T(8,128)}, u32[]{:S(2)}) copy-start(f32[5,1000]{1,0:T(8,128)} %copy-done.3) | copy-start | bytes 60004
  654.1 88.5 %copy-start.6 = (f32[32,128]{1,0:T(8,128)S(1)}, f32[32,128]{1,0:T(8,128)}, u32[]{:S(2)}) copy-start(f32[32,128]{1,0:T(8,128)} %param.3) | copy-start | bytes 49156
  654.1 88.5 %copy-start.8 = (f32[1000]{0:T(1024)S(1)}, f32[1000]{0:T(1024)}, u32[]{:S(2)}) copy-start(f32[1000]{0:T(1024)} %copy-done.7) | copy-start | bytes 12004
  654.1 88.5 %copy-start.10 = (f32[1000]{0:T(1024)S(1)}, f32[1000]{0:T(1024)}, u32[]{:S(2)}) copy-start(f32[1000]{0:T(1024)} %copy-done.9) | copy-start | bytes 12004
  654.1 88.5 %copy-start.12 = (f32[1000]{0:T(1024)S(1)}, f32[1000]{0:T(1024)}, u32[]{:S(2)}) copy-start(f32[1000]{0:T(1024)} %copy-done.11) | copy-start | bytes 12004
Sparse Core Ops, SparseCore 0:
  319.2 71.4 all-reduce.2
  672.0 68.9 all-reduce.4
where the time goes:
time: 782 us; the launch traced here: 771 us
  local copies, waits for them, and re-layouts  320 us (41%)
  other arithmetic  252 us (32%)
  waiting for transfers between devices  143 us (18%)
  matrix products  35.6 us (5%)
  between operations  14.1 us (2%)
    sub x2, other arithmetic, running(): return center - time_step * flux  226 us
    psum x2, waiting for transfers between devices, body(): params = parameters(lax.psum(partial_sum, 'vert'))  141 us
    slice x4, local copies, waits for them, and re-layouts, below(): jnp.roll(center, offset, 2)  72.6 us
    slice x4, local copies, waits for them, and re-layouts, above(): jnp.roll(center, -offset, 2)  59 us
    unnamed x38, local copies, waits for them, and re-layouts  38 us
    slice x5, local copies, waits for them, and re-layouts, with_halo(): lax.slice_in_dim(cells, cells.shape[dim] - width, cells.shape[dim], axis=...  37.2 us
    dot_general x2, matrix products, body(): partial_sum = jnp.dot(table, moved, precision=lax.Precision.HIGHEST)  35.6 us
    sub x2, local copies, waits for them, and re-layouts, running(): return center - time_step * flux  34.7 us
  transfers between devices with their start and end apart: 10, of which 3 were waited for; matrix products, arithmetic and copies ran while one was open for 26% of the time, Pallas kernels for 0%

commit v1 on v0

v1 whole, which is shorter than its diff:
```python
import functools
import math

import jax
import jax.numpy as jnp
from jax import lax
from jax.experimental import pallas as pl
from jax.experimental.pallas import tpu as pltpu
from jax.sharding import PartitionSpec as P

VG = 20
NZ = 2
SPEED_MAX = 4.5
DT = 0.3 / 4.5
STEP = 2.0 * SPEED_MAX / VG
WEIGHT = STEP**3 / (2.0 * math.pi) ** 1.5
MESH = pl.DeviceIdType.MESH
HALF = VG // 2
SLAB = 4
PAD = 8


def speed_of(index):
    if isinstance(index, int):
        return STEP * (index + 0.5) - SPEED_MAX
    return STEP * (index.astype(jnp.float32) + 0.5) - SPEED_MAX


def group_place(first, group, size):
    start = first + group * size
    last = 0 if size == VG else lax.rem(start, VG)
    return start // (VG * VG), lax.rem(start // VG, VG), last


def amplitudes(ramp, flow_x, flow_y, inv, cx, cy):
    dx = cx - flow_x
    dy = cy - flow_y
    return ramp * jnp.exp(-inv * (dx * dx + dy * dy))


def stream(n_vert, size, chunk_groups, dist, rate, out, par_out, state, xs1, xh1, xs2, xh2, ys1, yh1, ys2, yh2,
           acc, mom, rs, pslab, ag, par, ez, hps, hpr, ezh, load_sem, out_sem,
           xs1_s, xs1_r, xs2_s, xs2_r, ys1_s, ys1_r, ys2_s, ys2_r, rs_s, rs_r, ag_s, ag_r, hp_s, hp_r):
    count, rows, cols = dist.shape
    groups = count // size
    chunks = groups // chunk_groups
    chunk_vel = chunk_groups * size
    owners = rows // SLAB
    gx, gy, me = lax.axis_index("gx"), lax.axis_index("gy"), lax.axis_index("vert")
    to_x = {"gx": 1 - gx}
    to_y = {"gy": 1 - gy}
    first = me * count
    x_up = me * 2 >= n_vert
    lane = lax.broadcasted_iota(jnp.int32, (rows, cols), 1)
    even = lane % NZ == 0
    slot = lane // (2 * NZ)

    def load(c):
        part = pl.ds(c * chunk_vel, chunk_vel)
        return pltpu.make_async_copy(dist.at[part], state.at[part, pl.ds(0, rows)], load_sem.at[c])

    def store(c):
        part = pl.ds(c * chunk_vel, chunk_vel)
        return pltpu.make_async_copy(state.at[part, pl.ds(0, rows)], out.at[part], out_sem.at[c])

    def send(src, dst, s_sem, r_sem, c, device):
        part = pl.ds(c * chunk_groups, chunk_groups)
        return pltpu.make_async_remote_copy(
            src_ref=src.at[part], dst_ref=dst.at[part], send_sem=s_sem.at[c], recv_sem=r_sem.at[c],
            device_id=device, device_id_type=MESH)

    def each(n, fn, low=0):
        lax.fori_loop(low, n, lambda c, z: (fn(c), z)[1], 0)

    each(chunks, lambda c: load(c).start())

    barrier = pltpu.get_barrier_semaphore()
    pl.semaphore_signal(barrier, inc=1, device_id=to_x, device_id_type=MESH)
    pl.semaphore_signal(barrier, inc=1, device_id=to_y, device_id_type=MESH)
    each(n_vert, lambda k: pl.semaphore_signal(
        barrier, inc=1, device_id={"vert": lax.rem(me + k, n_vert)}, device_id_type=MESH), 1)
    pl.semaphore_wait(barrier, n_vert + 1)

    def pack_chunk(c):
        load(c).wait()

        def pack(n, z):
            g = c * chunk_groups + n
            _, j, _ = group_place(first, g, size)
            turn = jnp.where(j >= HALF, 2 * NZ, 0)
            packed = jnp.zeros((rows, cols), jnp.float32)
            for t in range(size):
                v = g * size + t
                f = state[v, 0:rows, :]
                packed = jnp.where(slot == t, pltpu.roll(f, 2 * NZ * t + turn, 1), packed)
                xs1[g, 2 * t : 2 * t + 2, :] = jnp.where(x_up, f[rows - 2 : rows], f[0:2])
            ys1[g] = packed
            return z

        lax.fori_loop(0, chunk_groups, pack, 0)
        send(xs1, xh1, xs1_s, xs1_r, c, to_x).start()
        send(ys1, yh1, ys1_s, ys1_r, c, to_y).start()

    each(chunks, pack_chunk)

    def move_group(g, up, xh, yh, xs):
        i, j, l0 = group_place(first, g, size)
        cx, cy = speed_of(i), speed_of(j)
        ax, ay = DT * jnp.abs(cx), DT * jnp.abs(cy)
        y_up = j >= HALF
        turn = jnp.where(y_up, 2 * NZ, 0)
        near = jnp.where(y_up, NZ, cols - NZ)
        far = jnp.where(y_up, 2 * NZ, cols - 2 * NZ)
        edge = lax.rem(lane + turn, cols)
        edge_near = jnp.where(y_up, edge - NZ, edge)
        in_far = edge < 2 * NZ
        in_near = (edge_near >= 0) & (edge_near < NZ)
        base = 1.0 - 1.5 * ax - 1.5 * ay
        halo = yh[g]
        a = b = d = jnp.zeros((rows, cols), jnp.float32)
        tall = rows + PAD
        at = tall - 2 if up else rows
        for t in range(size):
            v = g * size + t
            state[v, at : at + 2, :] = xh[g, 2 * t : 2 * t + 2, :]
        for t in range(size):
            v = g * size + t
            az = 2.0 * DT * (abs(speed_of(t)) if size == VG else jnp.abs(speed_of(l0 + t)))
            whole = state[v]
            f = whole[0:rows]
            near_x = pltpu.roll(whole, 1 if up else tall - 1, 0)[0:rows]
            far_x = pltpu.roll(whole, 2 if up else tall - 2, 0)[0:rows]
            other = jnp.where(even, pltpu.roll(f, cols - 1, 1), pltpu.roll(f, 1, 1))
            edge_f = pltpu.roll(halo, lax.rem(2 * cols - 2 * NZ * t - turn, cols), 1)
            near_y = pltpu.roll(jnp.where(in_near, edge_f, f), near, 1)
            far_y = pltpu.roll(jnp.where(in_far, edge_f, f), far, 1)
            m = (base - az) * f + (2.0 * ax) * near_x - (0.5 * ax) * far_x
            m = m + ((2.0 * ay) * near_y - (0.5 * ay) * far_y + az * other)
            state[v, 0:rows, :] = m
            if xs is not None:
                xs[g, 2 * t : 2 * t + 2, :] = m[rows - 2 : rows] if up else m[0:2]
            a = a + m
            b = b + a
            d = d + b
        e = speed_of(l0) + STEP * size
        acc[0] += a
        acc[1] += cx * a
        acc[2] += cy * a
        acc[3] += e * a - STEP * b
        acc[4] += (cx * cx + cy * cy + e * e) * a - (2.0 * STEP * e + STEP * STEP) * b + (2.0 * STEP * STEP) * d

    def reduce_moments(step):
        for o in range(owners):
            for p in range(5):
                mom[o, p] = acc[p, SLAB * o : SLAB * (o + 1), :]

        def to_owner(o):
            return pltpu.make_async_remote_copy(
                src_ref=mom.at[o], dst_ref=rs.at[step, me], send_sem=rs_s.at[step, o], recv_sem=rs_r.at[step, me],
                device_id={"vert": o}, device_id_type=MESH)

        def from_device(s):
            return pltpu.make_async_remote_copy(
                src_ref=mom.at[0], dst_ref=rs.at[step, s], send_sem=rs_s.at[step, 0], recv_sem=rs_r.at[step, s],
                device_id={"vert": s}, device_id_type=MESH)

        def spread(s):
            return pltpu.make_async_remote_copy(
                src_ref=pslab.at[step], dst_ref=ag.at[step, me], send_sem=ag_s.at[step, s],
                recv_sem=ag_r.at[step, me], device_id={"vert": s}, device_id_type=MESH)

        def from_owner(o):
            return pltpu.make_async_remote_copy(
                src_ref=pslab.at[step], dst_ref=ag.at[step, o], send_sem=ag_s.at[step, 0],
                recv_sem=ag_r.at[step, o], device_id={"vert": o}, device_id_type=MESH)

        def others_owning(fn):
            def one(k):
                o = lax.rem(me + k, n_vert)
                if n_vert <= owners:
                    fn(o)
                else:
                    pl.when(o < owners)(lambda: fn(o))
            each(n_vert, one, 1)

        def others(fn):
            each(n_vert, lambda k: fn(lax.rem(me + k, n_vert)), 1)

        others_owning(lambda o: to_owner(o).start())

        def own():
            others(lambda s: from_device(s).wait_recv())

            def add(k, total):
                return total + rs[step, lax.rem(me + k, n_vert)]

            total = lax.fori_loop(1, n_vert, add, mom[me])
            mass = total[0]
            ux, uy, uz = total[1] / mass, total[2] / mass, total[3] / mass
            temper = (total[4] / mass - (ux * ux + uy * uy + uz * uz)) / 3.0
            pslab[step, 0] = WEIGHT * mass / (temper * jnp.sqrt(temper))
            pslab[step, 1] = ux
            pslab[step, 2] = uy
            pslab[step, 3] = uz
            pslab[step, 4] = 0.5 / temper
            others(lambda s: spread(s).start())
            ag[step, me] = pslab[step]

        if n_vert <= owners:
            own()
        else:
            pl.when(me < owners)(own)
        others_owning(lambda o: from_owner(o).wait_recv())
        for o in range(owners):
            for p in range(5):
                par[p, SLAB * o : SLAB * (o + 1), :] = ag[step, o, p]
        others_owning(lambda o: to_owner(o).wait_send())
        if n_vert <= owners:
            others(lambda s: spread(s).wait_send())
        else:
            pl.when(me < owners)(lambda: others(lambda s: spread(s).wait_send()))

    def move_first(c):
        send(ys1, yh1, ys1_s, ys1_r, c, to_y).wait_recv()
        send(xs1, xh1, xs1_s, xs1_r, c, to_x).wait_recv()
        for up in (True, False):
            @pl.when(x_up if up else jnp.logical_not(x_up))
            def _():
                each(chunk_groups, lambda n: move_group(c * chunk_groups + n, up, xh1, yh1, xs2))
        send(xs2, xh2, xs2_s, xs2_r, c, to_x).start()

    acc[...] = jnp.zeros_like(acc)
    each(chunks, move_first)
    reduce_moments(0)

    keep = 1.0 - rate[...]
    ramp = rate[...] * par[0]
    for p, value in enumerate((keep, ramp, par[1], par[2], par[3], par[4])):
        two = jnp.where(x_up, value[rows - 2 : rows], value[0:2])
        for q in range(PAD // 2):
            hps[p, 2 * q : 2 * q + 2, :] = two
    edges = pltpu.make_async_remote_copy(
        src_ref=hps, dst_ref=hpr, send_sem=hp_s, recv_sem=hp_r, device_id=to_x, device_id_type=MESH)
    edges.start()

    def fill_ez(l):
        dz = speed_of(l) - par[3]
        ez[l] = jnp.exp(-par[4] * dz * dz)

    each(VG, fill_ez)

    def collide_chunk(c):
        def collide(n, z):
            g = c * chunk_groups + n
            i, j, l0 = group_place(first, g, size)
            turn = jnp.where(j >= HALF, 2 * NZ, 0)
            keep = 1.0 - rate[...]
            amp = amplitudes(rate[...] * par[0], par[1], par[2], par[4], speed_of(i), speed_of(j))
            packed = jnp.zeros((rows, cols), jnp.float32)
            for t in range(size):
                v = g * size + t
                f = keep * state[v, 0:rows, :] + amp * ez[l0 + t]
                state[v, 0:rows, :] = f
                packed = jnp.where(slot == t, pltpu.roll(f, 2 * NZ * t + turn, 1), packed)
            ys2[g] = packed
            return z

        lax.fori_loop(0, chunk_groups, collide, 0)
        send(ys2, yh2, ys2_s, ys2_r, c, to_y).start()

    each(chunks, collide_chunk)

    edges.wait_recv()
    packed_rows = xh2.shape[1]
    for s in range(VG // size):
        for q in range(packed_rows // PAD):
            index = s * size + (lax.broadcasted_iota(jnp.int32, (PAD, cols), 0) + PAD * q) // 2
            dz = speed_of(index) - hpr[4]
            ezh[s, PAD * q : PAD * (q + 1), :] = jnp.exp(-hpr[5] * dz * dz)

    def collide_edge(g):
        i, j, l0 = group_place(first, g, size)
        amp = amplitudes(hpr[1], hpr[2], hpr[3], hpr[5], speed_of(i), speed_of(j))
        for q in range(packed_rows // PAD):
            part = slice(PAD * q, PAD * (q + 1))
            xh2[g, part, :] = hpr[0] * xh2[g, part, :] + amp * ezh[l0 // size, part, :]

    def move_second(c):
        send(ys2, yh2, ys2_s, ys2_r, c, to_y).wait_recv()
        send(xs2, xh2, xs2_s, xs2_r, c, to_x).wait_recv()
        each(chunk_groups, lambda n: collide_edge(c * chunk_groups + n))
        for up in (True, False):
            @pl.when(x_up if up else jnp.logical_not(x_up))
            def _():
                each(chunk_groups, lambda n: move_group(c * chunk_groups + n, up, xh2, yh2, None))
        store(c).start()

    acc[...] = jnp.zeros_like(acc)
    each(chunks, move_second)
    reduce_moments(1)
    par_out[...] = par[...]

    def finish(c):
        store(c).wait()
        send(xs1, xh1, xs1_s, xs1_r, c, to_x).wait_send()
        send(xs2, xh2, xs2_s, xs2_r, c, to_x).wait_send()
        send(ys1, yh1, ys1_s, ys1_r, c, to_y).wait_send()
        send(ys2, yh2, ys2_s, ys2_r, c, to_y).wait_send()

    each(chunks, finish)
    edges.wait_send()


def relax(size, chunk_groups, moved, rate, par, out, ez):
    step = pl.program_id(0)
    first = lax.axis_index("vert") * (pl.num_programs(0) * chunk_groups * size)

    @pl.when(step == 0)
    def _():
        def fill(l, z):
            dz = speed_of(l) - par[3]
            ez[l] = jnp.exp(-par[4] * dz * dz)
            return z
        lax.fori_loop(0, VG, fill, 0)

    def one(n, z):
        i, j, l0 = group_place(first, step * chunk_groups + n, size)
        keep = 1.0 - rate[...]
        amp = amplitudes(rate[...] * par[0], par[1], par[2], par[4], speed_of(i), speed_of(j))
        for t in range(size):
            out[n * size + t] = keep * moved[n * size + t] + amp * ez[l0 + t]
        return z

    lax.fori_loop(0, chunk_groups, one, 0)


def body(mesh, distribution, collision_rate):
    count, rows, cols = distribution.shape
    n_vert = mesh.shape["vert"]
    size = math.gcd(count, VG)
    groups = count // size
    chunk_groups = math.gcd(groups, 5)
    chunks = groups // chunk_groups
    packed_rows = -(-2 * size // PAD) * PAD
    owners = rows // SLAB
    f32 = jnp.float32
    x_edge = pltpu.VMEM((groups, packed_rows, cols), f32)
    y_edge = pltpu.VMEM((groups, rows, cols), f32)
    dma = pltpu.SemaphoreType.DMA
    vmem = pl.BlockSpec(memory_space=pltpu.VMEM)
    anywhere = pl.BlockSpec(memory_space=pl.ANY)
    moved, par = pl.pallas_call(
        functools.partial(stream, n_vert, size, chunk_groups),
        out_shape=(jax.ShapeDtypeStruct(distribution.shape, f32), jax.ShapeDtypeStruct((5, rows, cols), f32)),
        in_specs=[anywhere, vmem],
        out_specs=(anywhere, vmem),
        scratch_shapes=[
            pltpu.VMEM((count, rows + PAD, cols), f32),
            x_edge, x_edge, x_edge, x_edge,
            y_edge, y_edge, y_edge, y_edge,
            pltpu.VMEM((5, rows, cols), f32),
            pltpu.VMEM((owners, 5, SLAB, cols), f32),
            pltpu.VMEM((2, n_vert, 5, SLAB, cols), f32),
            pltpu.VMEM((2, 5, SLAB, cols), f32),
            pltpu.VMEM((2, owners, 5, SLAB, cols), f32),
            pltpu.VMEM((5, rows, cols), f32),
            pltpu.VMEM((VG, rows, cols), f32),
            pltpu.VMEM((6, PAD, cols), f32),
            pltpu.VMEM((6, PAD, cols), f32),
            pltpu.VMEM((VG // size, packed_rows, cols), f32),
        ]
        + [dma((chunks,))] * 10
        + [dma((2, owners)), dma((2, n_vert)), dma((2, n_vert)), dma((2, owners)), dma, dma],
        compiler_params=pltpu.CompilerParams(
            collective_id=0, has_side_effects=True, vmem_limit_bytes=56 * 1024 * 1024),
        name="stream",
    )(distribution, collision_rate)
    block = pl.BlockSpec((chunk_groups * size, rows, cols), lambda c: (c, 0, 0))
    return pl.pallas_call(
        functools.partial(relax, size, chunk_groups),
        out_shape=jax.ShapeDtypeStruct(distribution.shape, f32),
        grid=(chunks,),
        in_specs=[block, vmem, vmem],
        out_specs=block,
        scratch_shapes=[pltpu.VMEM((VG, rows, cols), f32)],
        compiler_params=pltpu.CompilerParams(vmem_limit_bytes=32 * 1024 * 1024),
        name="relax",
    )(moved, collision_rate, par)


def solution(mesh):
    placed = (P("vert", "gx", "gy"), P("gx", "gy"))
    return jax.shard_map(
        functools.partial(body, mesh), mesh=mesh, in_specs=placed, out_specs=P("vert", "gx", "gy"), check_vma=False)
```

time: 782 us -> 191 us (0.24); the launches traced: 771 us -> 190 us
  local copies, waits for them, and re-layouts: 320 us -> 6.54 us
  other arithmetic: 252 us -> 0 us
  Pallas kernels: 0 us -> 184 us
  waiting for transfers between devices: 143 us -> 0 us
  matrix products: 35.6 us -> 0 us
  between operations: 14.1 us -> 0.03 us
    sub x2 -> x0, other arithmetic: 226 us -> none  [running(): return center - time_step * flux]
    pallas_call x0 -> x2, Pallas kernels: none -> 184 us  [the longest x1 175 us: body(): pl.pallas_call(functools.partial(stream, n_vert, size, chunk_groups), out...]
    slice x14 -> x0, local copies, waits for them, and re-layouts: 179 us -> none  [the longest x4 72.6 us: below(): jnp.roll(center, offset, 2)]
    psum x2 -> x0, waiting for transfers between devices: 141 us -> none  [body(): params = parameters(lax.psum(partial_sum, 'vert'))]
    ppermute x4 -> x0, local copies, waits for them, and re-layouts: 38.7 us -> none  [the longest x2 19.4 us: with_halo(): lax.ppermute(tail, axis, [(i, (i + 1) % count) for i in range(count)])]
    dot_general x2 -> x0, matrix products: 35.6 us -> none  [body(): partial_sum = jnp.dot(table, moved, precision=lax.Precision.HIGHEST)]
    sub x2 -> x0, local copies, waits for them, and re-layouts: 34.7 us -> none  [running(): return center - time_step * flux]
    unnamed x38 -> x6, local copies, waits for them, and re-layouts: 38 us -> 6.54 us
  transfers between devices with their start and end apart: 10 -> 0, of which waited for: 3 -> 0; matrix products, arithmetic and copies ran while one was open for 26% -> 0% of each run, Pallas kernels for 0% -> 0%
where the time goes in v1:
time: 191 us; the launch traced here: 190 us
  Pallas kernels  184 us (96%)
  local copies, waits for them, and re-layouts  6.54 us (3%)
    pallas_call x1, Pallas kernels, body(): pl.pallas_call(functools.partial(stream, n_vert, size, chunk_groups), out...  175 us
    pallas_call x1, Pallas kernels, body(): pl.pallas_call(functools.partial(relax, size, chunk_groups), out_shape=ja...  8.28 us
    unnamed x6, local copies, waits for them, and re-layouts  6.54 us

profile of v1, /device:TPU:0, one launch (start us, length us, event | category | flops | bytes accessed | tf_op | source)
XLA Modules:
  0.0 190.3 jit_solution(1764680816598210165)
XLA Ops:
  0.0 0.0 copy-start.2
  0.0 175.5 %stream.1 = (f32[1000,32,128]{2,1,0:T(8,128)}, f32[5,32,128]{2,1,0:T(8,128)}) custom-call(f32[1000,32,128]{2,1,0:T(8,128)} %dist.1, f32[32,128]{1,0:T(8,128)} %rate.3), custom_call_target="tpu_custom_call" | custom-call | tf_op jit(solution)/shard_map/stream/pallas_call | solution.py:352
  175.5 0.0 copy-done.2
  175.5 0.0 copy-start
  175.5 5.6 %copy-done = f32[1000,32,128]{2,1,0:T(8,128)S(1)} copy-done((f32[1000,32,128]{2,1,0:T(8,128)S(1)}, f32[1000,32,128]{2,1,0:T(8,128)}, u32[]{:S(2)}) %copy-start) | copy-done | bytes 16384024
  181.1 0.0 copy-start.1
  181.1 0.9 copy-done.1
  182.0 8.3 %relax.1 = f32[1000,32,128]{2,1,0:T(8,128)} custom-call(f32[1000,32,128]{2,1,0:T(8,128)S(1)} %copy-done, f32[32,128]{1,0:T(8,128)S(1)} %copy-done.2, f32[5,32,128]{2,1,0:T(8,128)S(1)} %copy-done.1), custom_call_target="tpu_custom_call" | custom-call | tf_op jit(solution)/shard_map/relax/pallas_call | solution.py:379
Async XLA Ops:
  0.0 175.5 %copy-start.2 = (f32[32,128]{1,0:T(8,128)S(1)}, f32[32,128]{1,0:T(8,128)}, u32[]{:S(2)}) copy-start(f32[32,128]{1,0:T(8,128)} %rate.3) | copy-start | bytes 49156
  175.5 5.7 %copy-start = (f32[1000,32,128]{2,1,0:T(8,128)S(1)}, f32[1000,32,128]{2,1,0:T(8,128)}, u32[]{:S(2)}) copy-start(f32[1000,32,128]{2,1,0:T(8,128)} %get-tuple-element.7.moved) | copy-start | bytes 49152004
  181.1 0.9 copy-start.1

commit v2 on v1

--- a/solution.py
+++ b/solution.py
@@ -18,6 +18,9 @@
 HALF = VG // 2
 SLAB = 4
 PAD = 8
+SUB = 8
+CHUNK = VG * VG // 2
+BLOCK = 4
 
 
 def speed_of(index):
@@ -311,6 +314,376 @@
     edges.wait_send()
 
 
+def stream_rows(n_vert, dist, rate, out, par_out, T, U, ys1, yh1, ys2, yh2, tab, acc, mom, rs, pslab, ag, par, ez, ey,
+                amp, hps, hpr, load_sem, out_sem, xs1_s, xs1_r, xs2_s, xs2_r, ys1_s, ys1_r, ys2_s, ys2_r,
+                rs_s, rs_r, ag_s, ag_r, hp_s, hp_r):
+    count, rows, cols = dist.shape
+    chunks = count // CHUNK
+    per_chunk = CHUNK // SUB
+    gx, gy, me = lax.axis_index("gx"), lax.axis_index("gy"), lax.axis_index("vert")
+    to_x = {"gx": 1 - gx}
+    to_y = {"gy": 1 - gy}
+    first = me * count
+    x_up = me * 2 >= n_vert
+    sign = jnp.where(x_up, 1, -1)
+    start = jnp.where(x_up, 2, rows + 1)
+    edge_from = jnp.where(x_up, rows, 2)
+    edge_to = jnp.where(x_up, 0, rows + 2)
+    lane = lax.broadcasted_iota(jnp.int32, (SUB, cols), 1)
+    sub = lax.broadcasted_iota(jnp.int32, (SUB, cols), 0)
+    even = lane % NZ == 0
+    slot = lane // (2 * NZ)
+
+    def row(k):
+        return start + sign * k
+
+    def each(n, fn, low=0):
+        lax.fori_loop(low, n, lambda c, z: (fn(c), z)[1], 0)
+
+    def span(c):
+        return pl.ds(c * CHUNK, CHUNK)
+
+    def load_start(c):
+        each(rows, lambda x: pltpu.make_async_copy(
+            dist.at[span(c), x, :], T.at[x + 2, span(c), :], load_sem.at[c]).start())
+
+    def load_wait(c):
+        inner = (pl.ds(2, rows), span(c))
+        pltpu.make_async_copy(U.at[inner], T.at[inner], load_sem.at[c]).wait()
+
+    def store_start(c):
+        each(rows, lambda x: pltpu.make_async_copy(
+            U.at[x + 2, span(c), :], out.at[span(c), x, :], out_sem.at[c]).start())
+
+    def store_wait(c):
+        inner = (pl.ds(2, rows), span(c))
+        pltpu.make_async_copy(U.at[inner], T.at[inner], out_sem.at[c]).wait()
+
+    def send_x(buf, s_sem, r_sem, c):
+        return pltpu.make_async_remote_copy(
+            src_ref=buf.at[pl.ds(edge_from, 2), span(c)], dst_ref=buf.at[pl.ds(edge_to, 2), span(c)],
+            send_sem=s_sem.at[c], recv_sem=r_sem.at[c], device_id=to_x, device_id_type=MESH)
+
+    def send_y(src, dst, s_sem, r_sem, c):
+        part = pl.ds(c * per_chunk, per_chunk)
+        return pltpu.make_async_remote_copy(
+            src_ref=src.at[part], dst_ref=dst.at[part], send_sem=s_sem.at[c], recv_sem=r_sem.at[c],
+            device_id=to_y, device_id_type=MESH)
+
+    def chunk_place(c):
+        begin = first + c * CHUNK
+        return begin // (VG * VG), lax.rem(begin // CHUNK, 2)
+
+    def by_half(half, fn):
+        for up in (True, False):
+            pl.when(half == (1 if up else 0))(functools.partial(fn, up))
+
+    each(chunks, load_start)
+
+    barrier = pltpu.get_barrier_semaphore()
+    pl.semaphore_signal(barrier, inc=1, device_id=to_x, device_id_type=MESH)
+    pl.semaphore_signal(barrier, inc=1, device_id=to_y, device_id_type=MESH)
+    each(n_vert, lambda k: pl.semaphore_signal(
+        barrier, inc=1, device_id={"vert": lax.rem(me + k, n_vert)}, device_id_type=MESH), 1)
+
+    def fill_table(g):
+        spot = (g * SUB + sub).astype(jnp.float32)
+        j = jnp.floor((spot + 0.5) * (1.0 / VG))
+        cy = STEP * (j + 0.5) - SPEED_MAX
+        cz = STEP * (spot - VG * j + 0.5) - SPEED_MAX
+        ay, az = DT * jnp.abs(cy), DT * jnp.abs(cz)
+        tab[g, 0] = 1.0 - 1.5 * ay - 2.0 * az
+        tab[g, 1] = 2.0 * ay
+        tab[g, 2] = 2.0 * az
+        tab[g, 3] = cy
+        tab[g, 4] = cz
+        tab[g, 5] = cy * cy + cz * cz
+
+    each(2 * per_chunk, fill_table)
+    pl.semaphore_wait(barrier, n_vert + 1)
+
+    def pack_chunk(c):
+        load_wait(c)
+        send_x(T, xs1_s, xs1_r, c).start()
+        _, half = chunk_place(c)
+
+        def run(up):
+            def pack(n):
+                at = pl.ds(pl.multiple_of(c * CHUNK + n * SUB, SUB), SUB)
+                packed = jnp.zeros((SUB, cols), jnp.float32)
+                for k in range(rows):
+                    turned = pltpu.roll(T[row(k), at, :], (2 * NZ * k + (2 * NZ if up else 0)) % cols, 1)
+                    packed = jnp.where(slot == k, turned, packed)
+                ys1[c * per_chunk + n] = packed
+
+            each(per_chunk, pack)
+
+        by_half(half, run)
+        send_y(ys1, yh1, ys1_s, ys1_r, c).start()
+
+    each(chunks, pack_chunk)
+
+    def move_chunk(c, yh):
+        i, half = chunk_place(c)
+        cx = speed_of(i)
+        ax = DT * jnp.abs(cx)
+
+        def run(up):
+            turn = 2 * NZ if up else 0
+            near, far = (NZ, 2 * NZ) if up else (cols - NZ, cols - 2 * NZ)
+            in_near = lane >= cols - NZ if up else lane < NZ
+            in_far = lane >= cols - 2 * NZ if up else lane < 2 * NZ
+
+            def block(kb):
+                k0 = kb * BLOCK
+
+                def five(sb, sums):
+                    sums = list(sums)
+                    for q in range(5):
+                        n = sb * 5 + q
+                        at = pl.ds(pl.multiple_of(c * CHUNK + n * SUB, SUB), SUB)
+                        place = half * per_chunk + n
+                        f = [T[row(k0 + kk), at, :] for kk in range(-2, BLOCK)]
+                        c0 = tab[place, 0] - 1.5 * ax
+                        by, bz = tab[place, 1], tab[place, 2]
+                        cy, cz, cq = tab[place, 3], tab[place, 4], tab[place, 5]
+                        halo = yh[c * per_chunk + n]
+                        for kk in range(BLOCK):
+                            far_x, near_x, mid = f[kk], f[kk + 1], f[kk + 2]
+                            back = lax.rem(2 * cols - turn - 2 * NZ * (k0 + kk), cols)
+                            edge = pltpu.roll(halo, back, 1)
+                            near_y = pltpu.roll(jnp.where(in_near, edge, mid), near, 1)
+                            far_y = pltpu.roll(jnp.where(in_far, edge, mid), far, 1)
+                            other = jnp.where(even, pltpu.roll(mid, cols - 1, 1), pltpu.roll(mid, 1, 1))
+                            m = (c0 * mid + (2.0 * ax) * (near_x - 0.25 * far_x)) + (
+                                by * (near_y - 0.25 * far_y) + bz * other)
+                            U[row(k0 + kk), at, :] = m
+                            sums[4 * kk] = sums[4 * kk] + m
+                            sums[4 * kk + 1] = sums[4 * kk + 1] + cy * m
+                            sums[4 * kk + 2] = sums[4 * kk + 2] + cz * m
+                            sums[4 * kk + 3] = sums[4 * kk + 3] + cq * m
+                    return tuple(sums)
+
+                zero = jnp.zeros((SUB, cols), jnp.float32)
+                sums = lax.fori_loop(0, per_chunk // 5, five, (zero,) * (4 * BLOCK))
+                for kk in range(BLOCK):
+                    x = row(k0 + kk) - 2
+                    a, my, mz, mq = sums[4 * kk : 4 * kk + 4]
+                    acc[0, x] += a
+                    acc[1, x] += cx * a
+                    acc[2, x] += my
+                    acc[3, x] += mz
+                    acc[4, x] += (cx * cx) * a + mq
+
+            each(rows // BLOCK, block)
+
+        by_half(half, run)
+
+    def reduce_moments(step):
+        for o in range(n_vert):
+            for p in range(5):
+                mom[o, p] = jnp.sum(acc[p, SLAB * o : SLAB * (o + 1)], axis=1)
+
+        def to_owner(o):
+            return pltpu.make_async_remote_copy(
+                src_ref=mom.at[o], dst_ref=rs.at[step, me], send_sem=rs_s.at[step, o], recv_sem=rs_r.at[step, me],
+                device_id={"vert": o}, device_id_type=MESH)
+
+        def from_device(s):
+            return pltpu.make_async_remote_copy(
+                src_ref=mom.at[s], dst_ref=rs.at[step, s], send_sem=rs_s.at[step, s], recv_sem=rs_r.at[step, s],
+                device_id={"vert": s}, device_id_type=MESH)
+
+        def spread(s):
+            return pltpu.make_async_remote_copy(
+                src_ref=pslab.at[step], dst_ref=ag.at[step, me], send_sem=ag_s.at[step, s],
+                recv_sem=ag_r.at[step, me], device_id={"vert": s}, device_id_type=MESH)
+
+        def from_owner(o):
+            return pltpu.make_async_remote_copy(
+                src_ref=pslab.at[step], dst_ref=ag.at[step, o], send_sem=ag_s.at[step, o],
+                recv_sem=ag_r.at[step, o], device_id={"vert": o}, device_id_type=MESH)
+
+        def others(fn):
+            each(n_vert, lambda k: fn(lax.rem(me + k, n_vert)), 1)
+
+        others(lambda o: to_owner(o).start())
+        others(lambda s: from_device(s).wait_recv())
+        total = lax.fori_loop(1, n_vert, lambda k, t: t + rs[step, lax.rem(me + k, n_vert)], mom[me])
+        mass = total[0]
+        ux, uy, uz = total[1] / mass, total[2] / mass, total[3] / mass
+        temper = (total[4] / mass - (ux * ux + uy * uy + uz * uz)) / 3.0
+        pslab[step, 0] = WEIGHT * mass / (temper * jnp.sqrt(temper))
+        pslab[step, 1] = ux
+        pslab[step, 2] = uy
+        pslab[step, 3] = uz
+        pslab[step, 4] = 0.5 / temper
+        others(lambda s: spread(s).start())
+        ag[step, me] = pslab[step]
+        others(lambda o: from_owner(o).wait_recv())
+        others(lambda o: to_owner(o).wait_send())
+        others(lambda s: spread(s).wait_send())
+
+    def move_first(c):
+        send_y(ys1, yh1, ys1_s, ys1_r, c).wait_recv()
+        send_x(T, xs1_s, xs1_r, c).wait_recv()
+        move_chunk(c, yh1)
+        send_x(U, xs2_s, xs2_r, c).start()
+
+    acc[...] = jnp.zeros_like(acc)
+    each(chunks, move_first)
+    reduce_moments(0)
+
+    par[...] = jnp.ones_like(par)
+    par[0, 2 : rows + 2, :] = 1.0 - rate[...]
+    for o in range(n_vert):
+        at = slice(SLAB * o + 2, SLAB * (o + 1) + 2)
+        par[1, at, :] = rate[SLAB * o : SLAB * (o + 1), :] * ag[0, o, 0]
+        for p in range(1, 5):
+            par[p + 1, at, :] = ag[0, o, p]
+    for p in range(6):
+        hps[p] = jnp.where(x_up, par[p, rows : rows + 2, :], par[p, 2:4, :])
+    edges = pltpu.make_async_remote_copy(
+        src_ref=hps, dst_ref=hpr, send_sem=hp_s, recv_sem=hp_r, device_id=to_x, device_id_type=MESH)
+    edges.start()
+
+    def fill_ey():
+        def one(j):
+            dy = speed_of(j) - par[3]
+            ey[j] = jnp.exp(-par[5] * dy * dy)
+        each(VG, one)
+
+    def fill_ez(r):
+        for q in range(5):
+            dz = tab[q, 4] - par[4, pl.ds(r, 1), :]
+            ez[q, r] = jnp.exp(-par[5, pl.ds(r, 1), :] * dz * dz)
+
+    def fill_amp(c):
+        i, half = chunk_place(c)
+        dx = speed_of(i) - par[2]
+        front = par[1] * jnp.exp(-par[5] * dx * dx)
+        for j in range(VG // 2):
+            amp[j] = front * ey[half * (VG // 2) + j]
+
+    def collided(c, sb, r):
+        low = jnp.broadcast_to(amp[2 * sb, pl.ds(r, 1), :], (SUB, cols))
+        high = jnp.broadcast_to(amp[2 * sb + 1, pl.ds(r, 1), :], (SUB, cols))
+        keep = jnp.broadcast_to(par[0, pl.ds(r, 1), :], (SUB, cols))
+        mixed = jnp.where(sub < SUB // 2, low, high)
+        found = []
+        for q, front in enumerate((low, low, mixed, high, high)):
+            at = pl.ds(pl.multiple_of(c * CHUNK + (sb * 5 + q) * SUB, SUB), SUB)
+            f = keep * U[r, at, :] + front * ez[q, r]
+            T[r, at, :] = f
+            found.append(f)
+        return found
+
+    fill_ey()
+    each(rows, lambda x: fill_ez(x + 2))
+
+    def collide_chunk(c):
+        send_x(T, xs1_s, xs1_r, c).wait_send()
+        _, half = chunk_place(c)
+        fill_amp(c)
+
+        def run(up):
+            def five(sb):
+                def some(kb, packed):
+                    packed = list(packed)
+                    for kk in range(BLOCK):
+                        k = kb * BLOCK + kk
+                        turn = lax.rem(2 * NZ * k + (2 * NZ if up else 0), cols)
+                        here = slot == k
+                        for q, f in enumerate(collided(c, sb, row(k))):
+                            packed[q] = jnp.where(here, pltpu.roll(f, turn, 1), packed[q])
+                    return tuple(packed)
+
+                zero = jnp.zeros((SUB, cols), jnp.float32)
+                packed = lax.fori_loop(0, rows // BLOCK, some, (zero,) * 5)
+                for q in range(5):
+                    ys2[c * per_chunk + sb * 5 + q] = packed[q]
+
+            each(per_chunk // 5, five)
+
+        by_half(half, run)
+        send_y(ys2, yh2, ys2_s, ys2_r, c).start()
+
+    each(chunks, collide_chunk)
+
+    edges.wait_recv()
+    for p in range(6):
+        par[p, 0:2, :] = hpr[p]
+        par[p, rows + 2 : rows + 4, :] = hpr[p]
+    fill_ey()
+    each(2, lambda x: fill_ez(edge_to + x))
+
+    def move_second(c):
+        send_y(ys2, yh2, ys2_s, ys2_r, c).wait_recv()
+        send_x(U, xs2_s, xs2_r, c).wait_recv()
+        send_x(U, xs2_s, xs2_r, c).wait_send()
+        fill_amp(c)
+
+        def edge(sb):
+            collided(c, sb, edge_to)
+            collided(c, sb, edge_to + 1)
+
+        each(per_chunk // 5, edge)
+        move_chunk(c, yh2)
+        store_start(c)
+
+    acc[...] = jnp.zeros_like(acc)
+    each(chunks, move_second)
+    reduce_moments(1)
+    for o in range(n_vert):
+        for p in range(5):
+            par_out[p, SLAB * o : SLAB * (o + 1), :] = ag[1, o, p]
+
+    def finish(c):
+        store_wait(c)
+        send_y(ys1, yh1, ys1_s, ys1_r, c).wait_send()
+        send_y(ys2, yh2, ys2_s, ys2_r, c).wait_send()
+
+    each(chunks, finish)
+    edges.wait_send()
+
+
+def run_rows(n_vert, distribution, collision_rate):
+    count, rows, cols = distribution.shape
+    chunks, groups = count // CHUNK, count // SUB
+    f32 = jnp.float32
+    state = pltpu.VMEM((rows + 4, count, cols), f32)
+    y_edge = pltpu.VMEM((groups, SUB, cols), f32)
+    dma = pltpu.SemaphoreType.DMA
+    vmem = pl.BlockSpec(memory_space=pltpu.VMEM)
+    anywhere = pl.BlockSpec(memory_space=pl.ANY)
+    return pl.pallas_call(
+        functools.partial(stream_rows, n_vert),
+        out_shape=(jax.ShapeDtypeStruct(distribution.shape, f32), jax.ShapeDtypeStruct((5, rows, cols), f32)),
+        in_specs=[anywhere, vmem],
+        out_specs=(anywhere, vmem),
+        scratch_shapes=[
+            state, state, y_edge, y_edge, y_edge, y_edge,
+            pltpu.VMEM((2 * CHUNK // SUB, 6, SUB, cols), f32),
+            pltpu.VMEM((5, rows, SUB, cols), f32),
+            pltpu.VMEM((n_vert, 5, SLAB, cols), f32),
+            pltpu.VMEM((2, n_vert, 5, SLAB, cols), f32),
+            pltpu.VMEM((2, 5, SLAB, cols), f32),
+            pltpu.VMEM((2, n_vert, 5, SLAB, cols), f32),
+            pltpu.VMEM((6, rows + 4, cols), f32),
+            pltpu.VMEM((5, rows + 4, SUB, cols), f32),
+            pltpu.VMEM((VG, rows + 4, cols), f32),
+            pltpu.VMEM((VG // 2, rows + 4, cols), f32),
+            pltpu.VMEM((6, 2, cols), f32),
+            pltpu.VMEM((6, 2, cols), f32),
+        ]
+        + [dma((chunks,))] * 10
+        + [dma((2, n_vert))] * 4 + [dma, dma],
+        compiler_params=pltpu.CompilerParams(
+            collective_id=1, has_side_effects=True, vmem_limit_bytes=56 * 1024 * 1024),
+        name="stream_rows",
+    )(distribution, collision_rate)
+
+
 def relax(size, chunk_groups, moved, rate, par, out, ez):
     step = pl.program_id(0)
     first = lax.axis_index("vert") * (pl.num_programs(0) * chunk_groups * size)
@@ -349,32 +722,35 @@
     dma = pltpu.SemaphoreType.DMA
     vmem = pl.BlockSpec(memory_space=pltpu.VMEM)
     anywhere = pl.BlockSpec(memory_space=pl.ANY)
-    moved, par = pl.pallas_call(
-        functools.partial(stream, n_vert, size, chunk_groups),
-        out_shape=(jax.ShapeDtypeStruct(distribution.shape, f32), jax.ShapeDtypeStruct((5, rows, cols), f32)),
-        in_specs=[anywhere, vmem],
-        out_specs=(anywhere, vmem),
-        scratch_shapes=[
-            pltpu.VMEM((count, rows + PAD, cols), f32),
-            x_edge, x_edge, x_edge, x_edge,
-            y_edge, y_edge, y_edge, y_edge,
-            pltpu.VMEM((5, rows, cols), f32),
-            pltpu.VMEM((owners, 5, SLAB, cols), f32),
-            pltpu.VMEM((2, n_vert, 5, SLAB, cols), f32),
-            pltpu.VMEM((2, 5, SLAB, cols), f32),
-            pltpu.VMEM((2, owners, 5, SLAB, cols), f32),
-            pltpu.VMEM((5, rows, cols), f32),
-            pltpu.VMEM((VG, rows, cols), f32),
-            pltpu.VMEM((6, PAD, cols), f32),
-            pltpu.VMEM((6, PAD, cols), f32),
-            pltpu.VMEM((VG // size, packed_rows, cols), f32),
-        ]
-        + [dma((chunks,))] * 10
-        + [dma((2, owners)), dma((2, n_vert)), dma((2, n_vert)), dma((2, owners)), dma, dma],
-        compiler_params=pltpu.CompilerParams(
-            collective_id=0, has_side_effects=True, vmem_limit_bytes=56 * 1024 * 1024),
-        name="stream",
-    )(distribution, collision_rate)
+    if count % CHUNK == 0 and rows == SLAB * n_vert:
+        moved, par = run_rows(n_vert, distribution, collision_rate)
+    else:
+        moved, par = pl.pallas_call(
+            functools.partial(stream, n_vert, size, chunk_groups),
+            out_shape=(jax.ShapeDtypeStruct(distribution.shape, f32), jax.ShapeDtypeStruct((5, rows, cols), f32)),
+            in_specs=[anywhere, vmem],
+            out_specs=(anywhere, vmem),
+            scratch_shapes=[
+                pltpu.VMEM((count, rows + PAD, cols), f32),
+                x_edge, x_edge, x_edge, x_edge,
+                y_edge, y_edge, y_edge, y_edge,
+                pltpu.VMEM((5, rows, cols), f32),
+                pltpu.VMEM((owners, 5, SLAB, cols), f32),
+                pltpu.VMEM((2, n_vert, 5, SLAB, cols), f32),
+                pltpu.VMEM((2, 5, SLAB, cols), f32),
+                pltpu.VMEM((2, owners, 5, SLAB, cols), f32),
+                pltpu.VMEM((5, rows, cols), f32),
+                pltpu.VMEM((VG, rows, cols), f32),
+                pltpu.VMEM((6, PAD, cols), f32),
+                pltpu.VMEM((6, PAD, cols), f32),
+                pltpu.VMEM((VG // size, packed_rows, cols), f32),
+            ]
+            + [dma((chunks,))] * 10
+            + [dma((2, owners)), dma((2, n_vert)), dma((2, n_vert)), dma((2, owners)), dma, dma],
+            compiler_params=pltpu.CompilerParams(
+                collective_id=0, has_side_effects=True, vmem_limit_bytes=56 * 1024 * 1024),
+            name="stream",
+        )(distribution, collision_rate)
     block = pl.BlockSpec((chunk_groups * size, rows, cols), lambda c: (c, 0, 0))
     return pl.pallas_call(
         functools.partial(relax, size, chunk_groups),
@@ -383,7 +759,7 @@
         in_specs=[block, vmem, vmem],
         out_specs=block,
         scratch_shapes=[pltpu.VMEM((VG, rows, cols), f32)],
-        compiler_params=pltpu.CompilerParams(vmem_limit_bytes=32 * 1024 * 1024),
+        compiler_params=pltpu.CompilerParams(vmem_limit_bytes=60 * 1024 * 1024),
         name="relax",
     )(moved, collision_rate, par)
 

time: 191 us -> 172 us (0.901)
  Pallas kernels: 184 us -> 172 us
  local copies, waits for them, and re-layouts: 6.54 us -> 0 us
    pallas_call x1, Pallas kernels: 175 us -> 156 us  [run_rows(): pl.pallas_call(functools.partial(stream_rows, n_vert), out_shape=(jax.Sha...]
    pallas_call x1, Pallas kernels: 8.28 us -> 15.7 us  [body(): pl.pallas_call(functools.partial(relax, size, chunk_groups), out_shape=ja...]
    unnamed x6 -> x0, local copies, waits for them, and re-layouts: 6.54 us -> none
where the time goes in v2:
time: 172 us
  Pallas kernels  172 us (100%)
    pallas_call x1, Pallas kernels, run_rows(): pl.pallas_call(functools.partial(stream_rows, n_vert), out_shape=(jax.Sha...  156 us
    pallas_call x1, Pallas kernels, body(): pl.pallas_call(functools.partial(relax, size, chunk_groups), out_shape=ja...  15.7 us

profile of v2, /device:TPU:0, one launch (start us, length us, event | category | flops | bytes accessed | tf_op | source)
XLA Modules:
  0.0 171.8 jit_solution(16234708546697032174)
XLA Ops:
  0.0 156.1 %stream_rows.1 = (f32[1000,32,128]{2,1,0:T(8,128)}, f32[5,32,128]{2,1,0:T(8,128)}) custom-call(f32[1000,32,128]{2,1,0:T(8,128)} %dist.1, f32[32,128]{1,0:T(8,128)} %rate.3), custom_call_target="tpu_custom_call" | custom-call | tf_op jit(solution)/shard_map/stream_rows/pallas_call | solution.py:659
  156.1 15.7 %relax.1 = f32[1000,32,128]{2,1,0:T(8,128)} custom-call(f32[1000,32,128]{2,1,0:T(8,128)} %get-tuple-element.7.moved, f32[32,128]{1,0:T(8,128)} %rate.3, f32[5,32,128]{2,1,0:T(8,128)} %get-tuple-element.8.par), custom_call_target="tpu_custom_call" | custom-call | tf_op jit(solution)/shard_map/relax/pallas_call | solution.py:755

commit v3 on v2

--- a/solution.py
+++ b/solution.py
@@ -315,7 +315,7 @@
 
 
 def stream_rows(n_vert, dist, rate, out, par_out, T, U, ys1, yh1, ys2, yh2, tab, acc, mom, rs, pslab, ag, par, ez, ey,
-                amp, hps, hpr, load_sem, out_sem, xs1_s, xs1_r, xs2_s, xs2_r, ys1_s, ys1_r, ys2_s, ys2_r,
+                amp, hps, hpr, weights, load_sem, out_sem, xs1_s, xs1_r, xs2_s, xs2_r, ys1_s, ys1_r, ys2_s, ys2_r,
                 rs_s, rs_r, ag_s, ag_r, hp_s, hp_r):
     count, rows, cols = dist.shape
     chunks = count // CHUNK
@@ -331,7 +331,6 @@
     edge_to = jnp.where(x_up, 0, rows + 2)
     lane = lax.broadcasted_iota(jnp.int32, (SUB, cols), 1)
     sub = lax.broadcasted_iota(jnp.int32, (SUB, cols), 0)
-    even = lane % NZ == 0
     slot = lane // (2 * NZ)
 
     def row(k):
@@ -363,6 +362,12 @@
         return pltpu.make_async_remote_copy(
             src_ref=buf.at[pl.ds(edge_from, 2), span(c)], dst_ref=buf.at[pl.ds(edge_to, 2), span(c)],
             send_sem=s_sem.at[c], recv_sem=r_sem.at[c], device_id=to_x, device_id_type=MESH)
+
+    def send_first(n):
+        c, side = n // 2, lax.rem(n, 2)
+        return pltpu.make_async_remote_copy(
+            src_ref=dist.at[span(c), edge_from - 2 + side, :], dst_ref=T.at[edge_to + side, span(c), :],
+            send_sem=xs1_s.at[n], recv_sem=xs1_r.at[n], device_id=to_x, device_id_type=MESH)
 
     def send_y(src, dst, s_sem, r_sem, c):
         part = pl.ds(c * per_chunk, per_chunk)
@@ -400,11 +405,24 @@
         tab[g, 5] = cy * cy + cz * cz
 
     each(2 * per_chunk, fill_table)
+
+    def fill_weights():
+        source = lax.broadcasted_iota(jnp.int32, (cols, cols), 0)
+        target = lax.broadcasted_iota(jnp.int32, (cols, cols), 1)
+        swap = jnp.where(source == target + 1 - 2 * (target % NZ), 1.0, 0.0).astype(jnp.bfloat16)
+        for half, step in ((0, NZ), (1, -NZ)):
+            along = jnp.where(source == target + step, 1.0, jnp.where(source == target + 2 * step, -0.25, 0.0))
+            for part in range(2):
+                at = slice(part * cols, (part + 1) * cols)
+                weights[half, at, 0:cols] = along.astype(jnp.bfloat16)
+                weights[half, at, cols : 2 * cols] = swap
+
+    fill_weights()
     pl.semaphore_wait(barrier, n_vert + 1)
+    each(2 * chunks, lambda n: send_first(n).start())
 
     def pack_chunk(c):
         load_wait(c)
-        send_x(T, xs1_s, xs1_r, c).start()
         _, half = chunk_place(c)
 
         def run(up):
@@ -429,34 +447,44 @@
         ax = DT * jnp.abs(cx)
 
         def run(up):
-            turn = 2 * NZ if up else 0
-            near, far = (NZ, 2 * NZ) if up else (cols - NZ, cols - 2 * NZ)
-            in_near = lane >= cols - NZ if up else lane < NZ
-            in_far = lane >= cols - 2 * NZ if up else lane < 2 * NZ
+            outer = 0 if up else cols - 2 * NZ
+            in_edge = lane < 2 * NZ if up else lane >= outer
+            inside = lane % (2 * NZ)
+
+            def from_edges(g):
+                halo = yh[g]
+                if up:
+                    return jnp.where(inside < NZ, pltpu.roll(halo, cols - NZ, 1), 0.0) - 0.25 * halo
+                return jnp.where(inside >= NZ, pltpu.roll(halo, NZ, 1), 0.0) - 0.25 * halo
 
             def block(kb):
                 k0 = kb * BLOCK
 
                 def five(sb, sums):
                     sums = list(sums)
+                    at = pl.ds(pl.multiple_of(c * CHUNK + sb * 5 * SUB, SUB), 5 * SUB)
+                    f = [T[row(k0 + kk), at, :] for kk in range(-2, BLOCK)]
+                    mid = jnp.concatenate(f[2:], axis=0)
+                    high = mid.astype(jnp.bfloat16)
+                    low = (mid - high.astype(jnp.float32)).astype(jnp.bfloat16)
+                    mixed = jnp.dot(jnp.concatenate([high, low], axis=1), weights[1 if up else 0],
+                                    preferred_element_type=jnp.float32)
                     for q in range(5):
                         n = sb * 5 + q
                         at = pl.ds(pl.multiple_of(c * CHUNK + n * SUB, SUB), SUB)
                         place = half * per_chunk + n
-                        f = [T[row(k0 + kk), at, :] for kk in range(-2, BLOCK)]
                         c0 = tab[place, 0] - 1.5 * ax
                         by, bz = tab[place, 1], tab[place, 2]
                         cy, cz, cq = tab[place, 3], tab[place, 4], tab[place, 5]
-                        halo = yh[c * per_chunk + n]
+                        terms = from_edges(c * per_chunk + n)
+                        own = slice(q * SUB, (q + 1) * SUB)
                         for kk in range(BLOCK):
-                            far_x, near_x, mid = f[kk], f[kk + 1], f[kk + 2]
-                            back = lax.rem(2 * cols - turn - 2 * NZ * (k0 + kk), cols)
-                            edge = pltpu.roll(halo, back, 1)
-                            near_y = pltpu.roll(jnp.where(in_near, edge, mid), near, 1)
-                            far_y = pltpu.roll(jnp.where(in_far, edge, mid), far, 1)
-                            other = jnp.where(even, pltpu.roll(mid, cols - 1, 1), pltpu.roll(mid, 1, 1))
-                            m = (c0 * mid + (2.0 * ax) * (near_x - 0.25 * far_x)) + (
-                                by * (near_y - 0.25 * far_y) + bz * other)
+                            far_x, near_x, here = f[kk][own], f[kk + 1][own], f[kk + 2][own]
+                            back = lax.rem(outer + cols - 2 * NZ * (k0 + kk), cols)
+                            edge = jnp.where(in_edge, pltpu.roll(terms, back, 1), 0.0)
+                            got = slice((kk * 5 + q) * SUB, (kk * 5 + q + 1) * SUB)
+                            m = (c0 * here + (2.0 * ax) * (near_x - 0.25 * far_x)) + (
+                                by * (mixed[got, 0:cols] + edge) + bz * mixed[got, cols : 2 * cols])
                             U[row(k0 + kk), at, :] = m
                             sums[4 * kk] = sums[4 * kk] + m
                             sums[4 * kk + 1] = sums[4 * kk + 1] + cy * m
@@ -526,7 +554,8 @@
 
     def move_first(c):
         send_y(ys1, yh1, ys1_s, ys1_r, c).wait_recv()
-        send_x(T, xs1_s, xs1_r, c).wait_recv()
+        send_first(2 * c).wait_recv()
+        send_first(2 * c + 1).wait_recv()
         move_chunk(c, yh1)
         send_x(U, xs2_s, xs2_r, c).start()
 
@@ -582,7 +611,6 @@
     each(rows, lambda x: fill_ez(x + 2))
 
     def collide_chunk(c):
-        send_x(T, xs1_s, xs1_r, c).wait_send()
         _, half = chunk_place(c)
         fill_amp(c)
 
@@ -644,6 +672,7 @@
         send_y(ys2, yh2, ys2_s, ys2_r, c).wait_send()
 
     each(chunks, finish)
+    each(2 * chunks, lambda n: send_first(n).wait_send())
     edges.wait_send()
 
 
@@ -675,8 +704,9 @@
             pltpu.VMEM((VG // 2, rows + 4, cols), f32),
             pltpu.VMEM((6, 2, cols), f32),
             pltpu.VMEM((6, 2, cols), f32),
+            pltpu.VMEM((2, 2 * cols, 2 * cols), jnp.bfloat16),
         ]
-        + [dma((chunks,))] * 10
+        + [dma((chunks,))] * 2 + [dma((2 * chunks,))] * 2 + [dma((chunks,))] * 6
         + [dma((2, n_vert))] * 4 + [dma, dma],
         compiler_params=pltpu.CompilerParams(
             collective_id=1, has_side_effects=True, vmem_limit_bytes=56 * 1024 * 1024),
@@ -696,15 +726,12 @@
             return z
         lax.fori_loop(0, VG, fill, 0)
 
-    def one(n, z):
+    keep = 1.0 - rate[...]
+    for n in range(chunk_groups):
         i, j, l0 = group_place(first, step * chunk_groups + n, size)
-        keep = 1.0 - rate[...]
         amp = amplitudes(rate[...] * par[0], par[1], par[2], par[4], speed_of(i), speed_of(j))
         for t in range(size):
             out[n * size + t] = keep * moved[n * size + t] + amp * ez[l0 + t]
-        return z
-
-    lax.fori_loop(0, chunk_groups, one, 0)
 
 
 def body(mesh, distribution, collision_rate):

time: 172 us -> 163 us (0.948)
  Pallas kernels: 172 us -> 162 us
    pallas_call x1, Pallas kernels: 156 us -> 147 us  [run_rows(): pl.pallas_call(functools.partial(stream_rows, n_vert), out_shape=(jax.Sha...]
where the time goes in v3:
time: 163 us; the launch traced here: 162 us
  Pallas kernels  162 us (99%)
    pallas_call x1, Pallas kernels, run_rows(): pl.pallas_call(functools.partial(stream_rows, n_vert), out_shape=(jax.Sha...  147 us
    pallas_call x1, Pallas kernels, body(): pl.pallas_call(functools.partial(relax, size, chunk_groups), out_shape=ja...  15.3 us

profile of v3, /device:TPU:0, one launch (start us, length us, event | category | flops | bytes accessed | tf_op | source)
XLA Modules:
  0.0 162.2 jit_solution(7300693951240711929)
XLA Ops:
  0.0 146.9 %stream_rows.1 = (f32[1000,32,128]{2,1,0:T(8,128)}, f32[5,32,128]{2,1,0:T(8,128)}) custom-call(f32[1000,32,128]{2,1,0:T(8,128)} %dist.1, f32[32,128]{1,0:T(8,128)} %rate.3), custom_call_target="tpu_custom_call" | custom-call | tf_op jit(solution)/shard_map/stream_rows/pallas_call | solution.py:688
  146.9 15.3 %relax.1 = f32[1000,32,128]{2,1,0:T(8,128)} custom-call(f32[1000,32,128]{2,1,0:T(8,128)} %get-tuple-element.7.moved, f32[32,128]{1,0:T(8,128)} %rate.3, f32[5,32,128]{2,1,0:T(8,128)} %get-tuple-element.8.par), custom_call_target="tpu_custom_call" | custom-call | tf_op jit(solution)/shard_map/relax/pallas_call | solution.py:782

commit v4 on v3

--- a/solution.py
+++ b/solution.py
@@ -271,7 +271,7 @@
         lax.fori_loop(0, chunk_groups, collide, 0)
         send(ys2, yh2, ys2_s, ys2_r, c, to_y).start()
 
-    each(chunks, collide_chunk)
+    collide_chunk(0)
 
     edges.wait_recv()
     packed_rows = xh2.shape[1]
@@ -439,8 +439,6 @@
         by_half(half, run)
         send_y(ys1, yh1, ys1_s, ys1_r, c).start()
 
-    each(chunks, pack_chunk)
-
     def move_chunk(c, yh):
         i, half = chunk_place(c)
         cx = speed_of(i)
@@ -460,40 +458,33 @@
             def block(kb):
                 k0 = kb * BLOCK
 
-                def five(sb, sums):
-                    sums = list(sums)
-                    at = pl.ds(pl.multiple_of(c * CHUNK + sb * 5 * SUB, SUB), 5 * SUB)
-                    f = [T[row(k0 + kk), at, :] for kk in range(-2, BLOCK)]
-                    mid = jnp.concatenate(f[2:], axis=0)
-                    high = mid.astype(jnp.bfloat16)
-                    low = (mid - high.astype(jnp.float32)).astype(jnp.bfloat16)
-                    mixed = jnp.dot(jnp.concatenate([high, low], axis=1), weights[1 if up else 0],
-                                    preferred_element_type=jnp.float32)
-                    for q in range(5):
-                        n = sb * 5 + q
-                        at = pl.ds(pl.multiple_of(c * CHUNK + n * SUB, SUB), SUB)
-                        place = half * per_chunk + n
-                        c0 = tab[place, 0] - 1.5 * ax
-                        by, bz = tab[place, 1], tab[place, 2]
-                        cy, cz, cq = tab[place, 3], tab[place, 4], tab[place, 5]
-                        terms = from_edges(c * per_chunk + n)
-                        own = slice(q * SUB, (q + 1) * SUB)
-                        for kk in range(BLOCK):
-                            far_x, near_x, here = f[kk][own], f[kk + 1][own], f[kk + 2][own]
-                            back = lax.rem(outer + cols - 2 * NZ * (k0 + kk), cols)
-                            edge = jnp.where(in_edge, pltpu.roll(terms, back, 1), 0.0)
-                            got = slice((kk * 5 + q) * SUB, (kk * 5 + q + 1) * SUB)
-                            m = (c0 * here + (2.0 * ax) * (near_x - 0.25 * far_x)) + (
-                                by * (mixed[got, 0:cols] + edge) + bz * mixed[got, cols : 2 * cols])
-                            U[row(k0 + kk), at, :] = m
-                            sums[4 * kk] = sums[4 * kk] + m
-                            sums[4 * kk + 1] = sums[4 * kk + 1] + cy * m
-                            sums[4 * kk + 2] = sums[4 * kk + 2] + cz * m
-                            sums[4 * kk + 3] = sums[4 * kk + 3] + cq * m
-                    return tuple(sums)
-
-                zero = jnp.zeros((SUB, cols), jnp.float32)
-                sums = lax.fori_loop(0, per_chunk // 5, five, (zero,) * (4 * BLOCK))
+                f = [T[row(k0 + kk), span(c), :] for kk in range(-2, BLOCK)]
+                mid = jnp.concatenate(f[2:], axis=0)
+                high = mid.astype(jnp.bfloat16)
+                low = (mid - high.astype(jnp.float32)).astype(jnp.bfloat16)
+                mixed = jnp.dot(jnp.concatenate([high, low], axis=1), weights[1 if up else 0],
+                                preferred_element_type=jnp.float32)
+                sums = [jnp.zeros((SUB, cols), jnp.float32)] * (4 * BLOCK)
+                for n in range(per_chunk):
+                    at = pl.ds(pl.multiple_of(c * CHUNK + n * SUB, SUB), SUB)
+                    place = half * per_chunk + n
+                    c0 = tab[place, 0] - 1.5 * ax
+                    by, bz = tab[place, 1], tab[place, 2]
+                    cy, cz, cq = tab[place, 3], tab[place, 4], tab[place, 5]
+                    terms = from_edges(c * per_chunk + n)
+                    own = slice(n * SUB, (n + 1) * SUB)
+                    for kk in range(BLOCK):
+                        far_x, near_x, here = f[kk][own], f[kk + 1][own], f[kk + 2][own]
+                        back = lax.rem(outer + cols - 2 * NZ * (k0 + kk), cols)
+                        edge = jnp.where(in_edge, pltpu.roll(terms, back, 1), 0.0)
+                        got = slice(kk * CHUNK + n * SUB, kk * CHUNK + (n + 1) * SUB)
+                        m = (c0 * here + (2.0 * ax) * (near_x - 0.25 * far_x)) + (
+                            by * (mixed[got, 0:cols] + edge) + bz * mixed[got, cols : 2 * cols])
+                        U[row(k0 + kk), at, :] = m
+                        sums[4 * kk] = sums[4 * kk] + m
+                        sums[4 * kk + 1] = sums[4 * kk + 1] + cy * m
+                        sums[4 * kk + 2] = sums[4 * kk + 2] + cz * m
+                        sums[4 * kk + 3] = sums[4 * kk + 3] + cq * m
                 for kk in range(BLOCK):
                     x = row(k0 + kk) - 2
                     a, my, mz, mq = sums[4 * kk : 4 * kk + 4]
@@ -553,6 +544,7 @@
         others(lambda s: spread(s).wait_send())
 
     def move_first(c):
+        pl.when(c + 1 < chunks)(lambda: pack_chunk(c + 1))
         send_y(ys1, yh1, ys1_s, ys1_r, c).wait_recv()
         send_first(2 * c).wait_recv()
         send_first(2 * c + 1).wait_recv()
@@ -560,6 +552,7 @@
         send_x(U, xs2_s, xs2_r, c).start()
 
     acc[...] = jnp.zeros_like(acc)
+    pack_chunk(0)
     each(chunks, move_first)
     reduce_moments(0)
 
@@ -618,8 +611,8 @@
             def five(sb):
                 def some(kb, packed):
                     packed = list(packed)
-                    for kk in range(BLOCK):
-                        k = kb * BLOCK + kk
+                    for kk in range(2 * BLOCK):
+                        k = kb * 2 * BLOCK + kk
                         turn = lax.rem(2 * NZ * k + (2 * NZ if up else 0), cols)
                         here = slot == k
                         for q, f in enumerate(collided(c, sb, row(k))):
@@ -627,7 +620,7 @@
                     return tuple(packed)
 
                 zero = jnp.zeros((SUB, cols), jnp.float32)
-                packed = lax.fori_loop(0, rows // BLOCK, some, (zero,) * 5)
+                packed = lax.fori_loop(0, rows // (2 * BLOCK), some, (zero,) * 5)
                 for q in range(5):
                     ys2[c * per_chunk + sb * 5 + q] = packed[q]
 
@@ -636,7 +629,7 @@
         by_half(half, run)
         send_y(ys2, yh2, ys2_s, ys2_r, c).start()
 
-    each(chunks, collide_chunk)
+    collide_chunk(0)
 
     edges.wait_recv()
     for p in range(6):
@@ -646,6 +639,7 @@
     each(2, lambda x: fill_ez(edge_to + x))
 
     def move_second(c):
+        pl.when(c + 1 < chunks)(lambda: collide_chunk(c + 1))
         send_y(ys2, yh2, ys2_s, ys2_r, c).wait_recv()
         send_x(U, xs2_s, xs2_r, c).wait_recv()
         send_x(U, xs2_s, xs2_r, c).wait_send()

time: 163 us -> 113 us (0.69)
  Pallas kernels: 162 us -> 112 us
    pallas_call x1, Pallas kernels: 147 us -> 96.9 us  [run_rows(): pl.pallas_call(functools.partial(stream_rows, n_vert), out_shape=(jax.Sha...]
where the time goes in v4:
time: 113 us; the launch traced here: 112 us
  Pallas kernels  112 us (99%)
    pallas_call x1, Pallas kernels, run_rows(): pl.pallas_call(functools.partial(stream_rows, n_vert), out_shape=(jax.Sha...  96.9 us
    pallas_call x1, Pallas kernels, body(): pl.pallas_call(functools.partial(relax, size, chunk_groups), out_shape=ja...  15.3 us

profile of v4, /device:TPU:0, one launch (start us, length us, event | category | flops | bytes accessed | tf_op | source)
XLA Modules:
  0.0 112.3 jit_solution(14529563257235334337)
XLA Ops:
  0.0 96.9 %stream_rows.1 = (f32[1000,32,128]{2,1,0:T(8,128)}, f32[5,32,128]{2,1,0:T(8,128)}) custom-call(f32[1000,32,128]{2,1,0:T(8,128)} %dist.1, f32[32,128]{1,0:T(8,128)} %rate.3), custom_call_target="tpu_custom_call" | custom-call | tf_op jit(solution)/shard_map/stream_rows/pallas_call | solution.py:682
  97.0 15.3 %relax.1 = f32[1000,32,128]{2,1,0:T(8,128)} custom-call(f32[1000,32,128]{2,1,0:T(8,128)} %get-tuple-element.7.moved, f32[32,128]{1,0:T(8,128)} %rate.3, f32[5,32,128]{2,1,0:T(8,128)} %get-tuple-element.8.par), custom_call_target="tpu_custom_call" | custom-call | tf_op jit(solution)/shard_map/relax/pallas_call | solution.py:776

commit v5 on v4

--- a/solution.py
+++ b/solution.py
@@ -609,18 +609,17 @@
 
         def run(up):
             def five(sb):
-                def some(kb, packed):
+                def some(packed):
                     packed = list(packed)
-                    for kk in range(2 * BLOCK):
-                        k = kb * 2 * BLOCK + kk
-                        turn = lax.rem(2 * NZ * k + (2 * NZ if up else 0), cols)
+                    for k in range(rows):
+                        turn = (2 * NZ * k + (2 * NZ if up else 0)) % cols
                         here = slot == k
                         for q, f in enumerate(collided(c, sb, row(k))):
                             packed[q] = jnp.where(here, pltpu.roll(f, turn, 1), packed[q])
                     return tuple(packed)
 
                 zero = jnp.zeros((SUB, cols), jnp.float32)
-                packed = lax.fori_loop(0, rows // (2 * BLOCK), some, (zero,) * 5)
+                packed = some((zero,) * 5)
                 for q in range(5):
                     ys2[c * per_chunk + sb * 5 + q] = packed[q]
 
@@ -780,7 +779,7 @@
         in_specs=[block, vmem, vmem],
         out_specs=block,
         scratch_shapes=[pltpu.VMEM((VG, rows, cols), f32)],
-        compiler_params=pltpu.CompilerParams(vmem_limit_bytes=60 * 1024 * 1024),
+        compiler_params=pltpu.CompilerParams(vmem_limit_bytes=32 * 1024 * 1024),
         name="relax",
     )(moved, collision_rate, par)
 

time: 113 us -> 107 us (0.947)
  Pallas kernels: 112 us -> 99.8 us
  local copies, waits for them, and re-layouts: 0 us -> 6.54 us
    pallas_call x1, Pallas kernels: 15.3 us -> 7.83 us  [body(): pl.pallas_call(functools.partial(relax, size, chunk_groups), out_shape=ja...]
    unnamed x0 -> x6, local copies, waits for them, and re-layouts: none -> 6.54 us
    pallas_call x1, Pallas kernels: 96.9 us -> 92 us  [run_rows(): pl.pallas_call(functools.partial(stream_rows, n_vert), out_shape=(jax.Sha...]
where the time goes in v5:
time: 107 us; the launch traced here: 106 us
  Pallas kernels  99.8 us (93%)
  local copies, waits for them, and re-layouts  6.54 us (6%)
    pallas_call x1, Pallas kernels, run_rows(): pl.pallas_call(functools.partial(stream_rows, n_vert), out_shape=(jax.Sha...  92 us
    pallas_call x1, Pallas kernels, body(): pl.pallas_call(functools.partial(relax, size, chunk_groups), out_shape=ja...  7.83 us
    unnamed x6, local copies, waits for them, and re-layouts  6.54 us

profile of v5, /device:TPU:0, one launch (start us, length us, event | category | flops | bytes accessed | tf_op | source)
XLA Modules:
  0.0 106.4 jit_solution(3198716228754594487)
XLA Ops:
  0.0 0.0 copy-start.2
  0.0 92.0 %stream_rows.1 = (f32[1000,32,128]{2,1,0:T(8,128)}, f32[5,32,128]{2,1,0:T(8,128)}) custom-call(f32[1000,32,128]{2,1,0:T(8,128)} %dist.1, f32[32,128]{1,0:T(8,128)} %rate.3), custom_call_target="tpu_custom_call" | custom-call | tf_op jit(solution)/shard_map/stream_rows/pallas_call | solution.py:681
  92.0 0.0 copy-done.2
  92.0 0.0 copy-start
  92.0 5.6 %copy-done = f32[1000,32,128]{2,1,0:T(8,128)S(1)} copy-done((f32[1000,32,128]{2,1,0:T(8,128)S(1)}, f32[1000,32,128]{2,1,0:T(8,128)}, u32[]{:S(2)}) %copy-start) | copy-done | bytes 16384024
  97.7 0.0 copy-start.1
  97.7 0.9 copy-done.1
  98.6 7.8 %relax.1 = f32[1000,32,128]{2,1,0:T(8,128)} custom-call(f32[1000,32,128]{2,1,0:T(8,128)S(1)} %copy-done, f32[32,128]{1,0:T(8,128)S(1)} %copy-done.2, f32[5,32,128]{2,1,0:T(8,128)S(1)} %copy-done.1), custom_call_target="tpu_custom_call" | custom-call | tf_op jit(solution)/shard_map/relax/pallas_call | solution.py:775
Async XLA Ops:
  0.0 92.0 %copy-start.2 = (f32[32,128]{1,0:T(8,128)S(1)}, f32[32,128]{1,0:T(8,128)}, u32[]{:S(2)}) copy-start(f32[32,128]{1,0:T(8,128)} %rate.3) | copy-start | bytes 49156
  92.0 5.7 %copy-start = (f32[1000,32,128]{2,1,0:T(8,128)S(1)}, f32[1000,32,128]{2,1,0:T(8,128)}, u32[]{:S(2)}) copy-start(f32[1000,32,128]{2,1,0:T(8,128)} %get-tuple-element.7.moved) | copy-start | bytes 49152004
  97.7 0.9 copy-start.1
